TPU v7x, 32 devices: a whole 2x2x4 slice. The times are simulated.
32 devices in a mesh: ctx: 8 (over z, x), sec: 2 (over y), dp: 2 (over core).
Axes of the slice: x: 2, y: 2, z: 4, core: 2. Of those that a mesh axis runs over, the one named last changes fastest.
Arguments:
- fresh_input: bfloat16 [2, 2048, 1536], P('dp', 'ctx'), may hold values from -6 to 6
- carried: bfloat16 [2, 2, 2048, 1536], P('sec', 'dp', 'ctx'), may hold values from -6 to 6
- qkv_weight: bfloat16 [2, 1536, 4608], P('sec', ('ctx', 'dp')), as said below
- out_weight: bfloat16 [2, 1536, 1536], P('sec', ('ctx', 'dp')), may hold values from -0.15625 to 0.15625
- rate_weight: bfloat16 [2, 1536, 6], P('sec', ('ctx', 'dp')), may hold values from -0.15625 to 0.15625
- fast_state: float32 [2, 2, 3, 6, 768, 256], P('sec', 'dp', None, None, 'ctx'), may hold values from -6 to 6
Outputs:
- passed: bfloat16 [2, 2, 2048, 1536], P('sec', 'dp', 'ctx')
- new_state: float32 [2, 2, 3, 6, 768, 256], P('sec', 'dp', None, None, 'ctx')
Inputs may be any that keep to these rules, and one draw needn't show every extreme that they name: Every entry of qkv_weight is at most 6 / sqrt(1536) in magnitude.
All inputs are finite; a program needn't handle non-finite values.
Results may differ from a plain program's by a relative error of at most 0.022.
Values may be sent and summed in bfloat16 or wider, within the bound.
A program may use at most 128 MiB of HBM per device.

v0:
```python
import jax
import jax.numpy as jnp
from jax import lax
from jax.sharding import PartitionSpec as P

NS_STEPS = 2


linear_coef = 3.4445
cubic_coef = -4.775
quintic_coef = 2.0315
update_scale = 8.0
highest = lax.Precision.HIGHEST


def from_behind(block, axis, distance):
    devices = range(lax.axis_size(axis))
    route = [(i - distance, i) for i in devices if i - distance in devices]
    return lax.ppermute(block, axis, route)


def swish(values):
    return values * jax.nn.sigmoid(values)


def unit_rows(values):
    return values / jnp.sqrt(jnp.sum(values * values, axis=-1, keepdims=True) + 1e-06)


def gram_local(current):
    return jnp.einsum("mhrd,mhre->mhde", current, current, precision=highest)


def local(fresh_input, carried, qkv_weight, out_weight, rate_weight, fast_state):
    received = from_behind(carried, "sec", 1)
    is_first = lax.axis_index("sec") == 0
    inputs = jnp.where(is_first, fresh_input[None], received)[0, 0]
    count = inputs.shape[0]
    heads = rate_weight.shape[2]
    head_dim = fast_state.shape[5]
    previous = fast_state[0, 0]
    gathered = lax.all_gather(previous.astype(jnp.bfloat16), "ctx", axis=2, tiled=True)
    full_qkv, full_out, full_rate = (
        lax.all_gather(qkv_weight[0], ("ctx", "dp"), axis=0, tiled=True),
        lax.all_gather(out_weight[0], ("ctx", "dp"), axis=0, tiled=True),
        lax.all_gather(rate_weight[0], ("ctx", "dp"), axis=0, tiled=True),
    )
    projected = jnp.dot(inputs, full_qkv, preferred_element_type=jnp.float32)
    rate_pre = jnp.dot(inputs, full_rate, preferred_element_type=jnp.float32)
    projected = projected.reshape(count, 3, heads, head_dim)
    query_rows = unit_rows(swish(projected[:, 0])).astype(jnp.bfloat16)
    key_rows = unit_rows(swish(projected[:, 1])).astype(jnp.bfloat16)
    value_rows = projected[:, 2].astype(jnp.bfloat16)
    rates = jax.nn.softplus(rate_pre)
    gate_fast, up_fast, down_fast = (gathered[0], gathered[1], gathered[2])
    gate_query = jnp.einsum(
        "thd,hfd->thf", query_rows, gate_fast, preferred_element_type=jnp.float32
    )
    up_query = jnp.einsum("thd,hfd->thf", query_rows, up_fast, preferred_element_type=jnp.float32)
    hidden = (swish(gate_query) * up_query).astype(jnp.bfloat16)
    mixture = jnp.einsum("thf,hfd->thd", hidden, down_fast, preferred_element_type=jnp.float32)
    head_out = (
        mixture * lax.rsqrt(jnp.mean(mixture * mixture, axis=-1, keepdims=True) + 1e-05)
    ).astype(jnp.bfloat16)
    head_out = head_out.reshape(count, heads * head_dim)
    branch_out = jnp.dot(head_out, full_out, preferred_element_type=jnp.float32)
    passed = (inputs.astype(jnp.float32) + branch_out).astype(jnp.bfloat16)
    gate_pre = jnp.einsum("thd,hfd->thf", key_rows, gate_fast, preferred_element_type=jnp.float32)
    up_pre = jnp.einsum("thd,hfd->thf", key_rows, up_fast, preferred_element_type=jnp.float32)
    sigma = jax.nn.sigmoid(gate_pre)
    gate_act = gate_pre * sigma
    key_hidden = (gate_act * up_pre).astype(jnp.bfloat16)
    scaled_values = (rates[:, :, None] * value_rows.astype(jnp.float32)).astype(jnp.bfloat16)
    hidden_grad = -jnp.einsum(
        "thd,hfd->thf", scaled_values, down_fast, preferred_element_type=jnp.float32
    )
    up_grad = (hidden_grad * gate_act).astype(jnp.bfloat16)
    gate_grad = (hidden_grad * up_pre * sigma * (1.0 + gate_pre * (1.0 - sigma))).astype(
        jnp.bfloat16
    )
    grad_gate = jnp.einsum("thf,thd->hfd", gate_grad, key_rows, preferred_element_type=jnp.float32)
    grad_up = jnp.einsum("thf,thd->hfd", up_grad, key_rows, preferred_element_type=jnp.float32)
    grad_down = -jnp.einsum(
        "thf,thd->hfd", key_hidden, scaled_values, preferred_element_type=jnp.float32
    )
    partial_value = jnp.stack([grad_gate, grad_up, grad_down])
    gradient = lax.psum_scatter(
        partial_value.astype(jnp.bfloat16), "ctx", scatter_dimension=2, tiled=True
    ).astype(jnp.float32)
    current = gradient
    for iteration in range(NS_STEPS):
        square = lax.psum(gram_local(current).astype(jnp.bfloat16), "ctx").astype(jnp.float32)
        if iteration == 0:
            inverse_norm = lax.rsqrt(jnp.trace(square, axis1=-2, axis2=-1) + 1e-06)[
                :, :, None, None
            ]
            current = current * inverse_norm
            square = square * inverse_norm * inverse_norm
        product = jnp.einsum("mhrd,mhde->mhre", current, square, precision=highest)
        current = (
            linear_coef * current
            + cubic_coef * product
            + quintic_coef * jnp.einsum("mhrd,mhde->mhre", product, square, precision=highest)
        )
    stepped = previous - update_scale * current
    rescale = jnp.sqrt(jnp.mean(previous * previous, axis=-1, keepdims=True) + 1e-06) * lax.rsqrt(
        jnp.mean(stepped * stepped, axis=-1, keepdims=True) + 1e-06
    )
    new_state = (stepped * rescale)[None, None]
    return (passed[None, None], new_state)


def solution(mesh):
    in_specs = (
        P("dp", "ctx", None),
        P("sec", "dp", "ctx", None),
        P("sec", ("ctx", "dp"), None),
        P("sec", ("ctx", "dp"), None),
        P("sec", ("ctx", "dp"), None),
        P("sec", "dp", None, None, "ctx", None),
    )
    out_specs = (P("sec", "dp", "ctx", None), P("sec", "dp", None, None, "ctx", None))
    return jax.shard_map(local, mesh=mesh, in_specs=in_specs, out_specs=out_specs, check_vma=False)
```

profile of v0, /device:TPU:24, one launch (start us, length us, event | category | flops | bytes accessed | tf_op | source)
XLA Modules:
  0.0 683.3 jit_solution(5050198175697575014)
XLA Ops:
  10.6 3.5 collective-permute-start
  14.3 24.0 %all-gather.2 = bf16[1,1536,6]{2,0,1:T(2,128)(2,1)S(1)} all-gather(bf16[1,96,6]{2,0,1:T(2,128)(2,1)S(1)} %copy.37), channel_id=4, replica_groups=mesh['ctx'=8,'sec'=2,'dp'=2] {'ctx','dp'}, dimensions={1}, use_global_device_ids=true | all-gather | bytes 19584 | tf_op jit(solution)/shard_map/all_gather | solution.py:46
  39.1 83.8 %all-gather.9.cloned.1.call-done = bf16[1,1536,4608]{2,1,0:T(8,128)(2,1)} async-done(((bf16[1,96,4608]{2,1,0:T(8,128)(2,1)}), bf16[1,1536,4608]{2,1,0:T(8,128)(2,1)}) %all-gather.9.cloned.1.call-update) | async-done | bytes 14155792 | tf_op jit(solution)/shard_map/all_gather | solution.py:44
  122.9 18.6 %copy.33 = bf16[4608,1536]{1,0:T(8,128)(2,1)} copy(bf16[4608,1536]{0,1:T(8,128)(2,1)} %bitcast.190) | data formatting | bytes 28311552 | tf_op jit(solution)/shard_map/dot_general | solution.py:48
  141.5 7.5 %fusion.53 = f32[256,3,6,256]{0,3,2,1:T(8,128)S(1)} fusion(bf16[3,6,256,1536]{3,2,1,0:T(8,128)(2,1)} %bitcast.191, bf16[1,1,256,1536]{3,2,1,0:T(8,128)(2,1)S(1)} %bitcast_select_fusion), kind=kOutput, calls=%fused_computation.78 | convolution fusion | flops 3623878656 | bytes 19660800 | tf_op jit(solution)/shard_map/dot_general | solution.py:48
  152.2 80.5 %all-gather.7.cloned.1.call-done = bf16[3,6,768,256]{3,2,1,0:T(8,128)(2,1)} async-done(((bf16[3,6,96,256]{3,2,1,0:T(8,128)(2,1)}), bf16[3,6,768,256]{3,2,1,0:T(8,128)(2,1)}) %all-gather.7.cloned.1.call-update) | async-done | bytes 7077904 | tf_op jit(solution)/shard_map/all_gather | solution.py:42
  232.7 5.7 fusion.34
  240.9 4.5 convert_bitcast_fusion
  245.4 3.2 fusion.36
  248.5 7.9 %convert_bitcast_fusion.1 = bf16[1,6,768,256]{3,2,1,0:T(8,128)(2,1)} fusion(f32[6,256,768]{2,1,0:T(8,128)} %fusion.34, f32[6,256,768]{2,1,0:T(8,128)} %fusion.36, f32[6,256,768]{2,1,0:T(8,128)S(1)} %fusion.37, f32[256,6]{0,1:T(8,128)S(1)} %add_sqrt_fusion, f32[256,3,6,256]{0,3,2,1:T(8,128)S(1)} %copy-done.3), kind=kOutput, calls=%fused_computation.41 | convolution fusion | flops 620494848 | bytes 18096128 | tf_op jit(solution)/shard_map/thf,thd->hfd/dot_general | solution.py:81
  256.4 5.7 fusion.21
  262.1 3.4 pad_maximum_fusion
  265.6 127.6 %reduce-scatter.2.cloned.1.call-done = bf16[3,6,96,256]{3,2,1,0:T(8,128)(2,1)} async-done(((bf16[3,6,768,256]{3,2,1,0:T(8,128)(2,1)}), bf16[3,6,96,256]{3,2,1,0:T(8,128)(2,1)}) %reduce-scatter.2.cloned.1.call-update) | async-done | bytes 884752 | tf_op jit(solution)/shard_map/reduce_scatter | solution.py:87
  393.1 3.8 convolution_convert_fusion.1
  399.4 5.2 fusion.35
  404.6 100.1 %all-reduce.3.cloned.1.call-done = bf16[3,6,256,256]{3,2,1,0:T(8,128)(2,1)} async-done(((bf16[3,6,256,256]{3,2,1,0:T(8,128)(2,1)}), bf16[3,6,256,256]{3,2,1,0:T(8,128)(2,1)}) %all-reduce.3.cloned.1.call-update) | async-done | bytes 2359312 | tf_op jit(solution)/shard_map/psum | solution.py:92
  507.1 5.5 fusion.4
  512.6 3.8 multiply_add_fusion
  516.4 5.5 convolution_convert_fusion
  522.0 8.5 %fusion.46 = (f32[256,6]{0,1:T(8,128)}, f32[6,256,256]{1,2,0:T(8,128)}) fusion(bf16[3,6,768,256]{3,2,1,0:T(8,128)(2,1)} %all-gather.7.cloned.1.call-done, f32[6,256,768]{2,1,0:T(8,128)} %fusion.35, f32[256,6]{0,1:T(8,128)} %copy-done.11, f32[256,3,6,256]{0,3,2,1:T(8,128)} %copy-done.2), kind=kOutput, calls=%fused_computation.66 | convolution fusion | flops 1218181632 | bytes 12597248 | tf_op jit(solution)/shard_map/thf,hfd->thd/dot_general | solution.py:61
  533.6 25.9 %all-gather.11.cloned.1.call-done = bf16[1,1536,1536]{2,1,0:T(8,128)(2,1)} async-done(((bf16[1,96,1536]{2,1,0:T(8,128)(2,1)}), bf16[1,1536,1536]{2,1,0:T(8,128)(2,1)}) %all-gather.11.cloned.1.call-update) | async-done | bytes 4718608 | tf_op jit(solution)/shard_map/all_gather | solution.py:45
  559.6 5.1 fusion.51
  564.6 105.3 %all-reduce.5.cloned.1.call-done = bf16[3,6,256,256]{3,2,1,0:T(8,128)(2,1)} async-done(((bf16[3,6,256,256]{3,2,1,0:T(8,128)(2,1)}), bf16[3,6,256,256]{3,2,1,0:T(8,128)(2,1)}) %all-reduce.5.cloned.1.call-update) | async-done | bytes 2359312 | tf_op jit(solution)/shard_map/psum | solution.py:92
  669.9 3.1 fusion.70
  (59 shorter events, 21.5 us)
Async XLA Ops:
  7.2 3.5 copy-start.13
  7.2 6.9 %copy-start.12 = (bf16[1,96,6]{1,2,0:T(8,128)(2,1)S(1)}, bf16[1,96,6]{1,2,0:T(8,128)(2,1)}, u32[]{:S(2)}) copy-start(bf16[1,96,6]{1,2,0:T(8,128)(2,1)} %param.10) | copy-start | bytes 3460
  7.2 115.7 %all-gather.9.cloned.1.call-start = ((), (), s32[]{:S(2)}) async-start(), calls=%async_computation.5 | async-start | bytes 15040512 | tf_op jit(solution)/shard_map/all_gather | solution.py:44
  7.9 30.8 %copy-start.10 = (bf16[1,256,1536]{2,1,0:T(8,128)(2,1)S(1)}, bf16[1,256,1536]{2,1,0:T(8,128)(2,1)}, u32[]{:S(2)}) copy-start(bf16[1,256,1536]{2,1,0:T(8,128)(2,1)} %param.6) | copy-start | bytes 2359300
  7.9 224.8 %all-gather.7.cloned.1.call-start = ((), (), s32[]{:S(2)}) async-start(), calls=%async_computation.1 | async-start | bytes 7962624 | tf_op jit(solution)/shard_map/all_gather | solution.py:42
  10.6 382.6 %reduce-scatter.2.cloned.1.call-start = ((), (), s32[]{:S(2)}) async-start(), calls=%async_computation.2 | async-start | bytes 7962624 | tf_op jit(solution)/shard_map/reduce_scatter | solution.py:87
  10.6 28.0 %collective-permute-start = (bf16[1,1,256,1536]{3,2,1,0:T(8,128)(2,1)S(1)}, bf16[1,1,256,1536]{3,2,1,0:T(8,128)(2,1)S(1)}, u32[]{:S(2)}, u32[]{:S(2)}) collective-permute-start(bf16[1,1,256,1536]{3,2,1,0:T(8,128)(2,1)S(1)} %copy-done.13), channel_id=1, source_target_pairs={{0,2},{1,3},{4,6},{5,7},{8,10},{9,11},{12,14},{13,15},{16,18},{17,... | collective-permute-start | bytes 2359304 | tf_op jit(solution)/shard_map/ppermute | solution.py:19
  38.8 102.7 %copy-start.6 = (bf16[1,1,256,1536]{3,2,1,0:T(8,128)(2,1)}, bf16[1,1,256,1536]{3,2,1,0:T(8,128)(2,1)S(1)}, u32[]{:S(2)}) copy-start(bf16[1,1,256,1536]{3,2,1,0:T(8,128)(2,1)S(1)} %bitcast_select_fusion) | copy-start | bytes 2359300
  149.0 2.2 copy-start.2
  232.7 5.7 copy-start.3
  232.7 7.3 %copy-start.9 = (bf16[3,6,768,256]{3,2,1,0:T(8,128)(2,1)S(1)}, bf16[3,6,768,256]{3,2,1,0:T(8,128)(2,1)}, u32[]{:S(2)}) copy-start(bf16[3,6,768,256]{3,2,1,0:T(8,128)(2,1)} %all-gather.7.cloned.1.call-done) | copy-start | bytes 21233668
  256.4 5.7 copy-start.7
  265.5 239.2 %all-reduce.3.cloned.1.call-start = ((), (), s32[]{:S(2)}) async-start(), calls=%async_computation.3 | async-start | bytes 4718592 | tf_op jit(solution)/shard_map/psum | solution.py:92
  396.9 1.5 copy-start
  396.9 162.6 %all-gather.11.cloned.1.call-start = ((), (), s32[]{:S(2)}) async-start(), calls=%async_computation.6 | async-start | bytes 5013504 | tf_op jit(solution)/shard_map/all_gather | solution.py:45
  397.5 272.4 %all-reduce.5.cloned.1.call-start = ((), (), s32[]{:S(2)}) async-start(), calls=%async_computation.4 | async-start | bytes 4718592 | tf_op jit(solution)/shard_map/psum | solution.py:92
  398.8 0.6 copy-start.11
  404.6 102.5 %copy-start.4 = (bf16[3,6,96,256]{3,2,1,0:T(8,128)(2,1)S(1)}, bf16[3,6,96,256]{3,2,1,0:T(8,128)(2,1)}, u32[]{:S(2)}) copy-start(bf16[3,6,96,256]{3,2,1,0:T(8,128)(2,1)} %reduce-scatter.2.cloned.1.call-done) | copy-start | bytes 2654212
  507.1 5.5 copy-start.5
  507.1 5.5 copy-start.8
  669.9 3.1 copy-start.1
Sparse Core Ops, SparseCore 0:
  10.3 112.5 all-gather.8
  125.7 106.9 all-gather.6
  265.7 127.4 reduce-scatter.1
  397.1 107.5 all-reduce.2
  506.8 52.6 all-gather.10
  563.0 106.8 all-reduce.4
where the time goes:
time: 688 us; the launch traced here: 683 us
  waiting for transfers between devices  524 us (76%)
  matrix products  77.9 us (11%)
  local copies, waits for them, and re-layouts  24.2 us (4%)
  blocking collectives  24 us (3%)
  other arithmetic  14.6 us (2%)
  between operations  14.3 us (2%)
    psum x2, waiting for transfers between devices, local(): lax.psum(gram_local(current).astype(jnp.bfloat16), 'ctx')  205 us
    reduce_scatter x1, waiting for transfers between devices, local(): lax.psum_scatter(partial_value.astype(jnp.bfloat16), 'ctx', scatter_dimen...  128 us
    all_gather x1, waiting for transfers between devices, local(): lax.all_gather(qkv_weight[0], ('ctx', 'dp'), axis=0, tiled=True)  83.8 us
    all_gather x1, waiting for transfers between devices, local(): lax.all_gather(previous.astype(jnp.bfloat16), 'ctx', axis=2, tiled=True)  80.5 us
    all_gather x1, waiting for transfers between devices, local(): lax.all_gather(out_weight[0], ('ctx', 'dp'), axis=0, tiled=True)  25.9 us
    all_gather x1, blocking collectives, local(): lax.all_gather(rate_weight[0], ('ctx', 'dp'), axis=0, tiled=True)  24 us
    dot_general x1, local copies, waits for them, and re-layouts, local(): projected = jnp.dot(inputs, full_qkv, preferred_element_type=jnp.float32)  18.6 us
  transfers between devices with their start and end apart: 7, of which 6 were waited for; matrix products, arithmetic and copies ran while one was open for 10% of the time, Pallas kernels for 0%

commit v1 on v0

v1 whole, which is shorter than its diff:
```python
import jax
import jax.numpy as jnp
from jax import lax
from jax.sharding import PartitionSpec as P

NS_STEPS = 2


linear_coef = 3.4445
cubic_coef = -4.775
quintic_coef = 2.0315
update_scale = 8.0
highest = lax.Precision.HIGHEST


def from_behind(block, axis, distance):
    devices = range(lax.axis_size(axis))
    route = [(i - distance, i) for i in devices if i - distance in devices]
    return lax.ppermute(block, axis, route)


def swish(values):
    return values * jax.nn.sigmoid(values)


def unit_rows(values):
    return values / jnp.sqrt(jnp.sum(values * values, axis=-1, keepdims=True) + 1e-06)


def head_slots(heads):
    devices = lax.axis_size("ctx")
    each = -(-heads // devices)
    return devices * each


def pad_axis(block, axis, size):
    widths = [(0, 0)] * block.ndim
    widths[axis] = (0, size - block.shape[axis])
    return jnp.pad(block, widths)


def exchange(block, split, concat):
    return lax.all_to_all(block, "ctx", split_axis=split, concat_axis=concat, tiled=True)


def matmul_tn(a, b, precision=None):
    return lax.dot_general(
        a, b, (((0,), (0,)), ((), ())), preferred_element_type=jnp.float32, precision=precision
    )


def orthogonalize(gradient):
    square = matmul_tn(gradient, gradient, highest)
    inverse_norm = lax.rsqrt(jnp.trace(square) + 1e-06)
    square = square * inverse_norm * inverse_norm
    eye = jnp.eye(square.shape[0], dtype=jnp.float32)
    total = None
    for iteration in range(NS_STEPS):
        quad = jnp.dot(square, square, precision=highest)
        poly = linear_coef * eye + cubic_coef * square + quintic_coef * quad
        total = poly if total is None else jnp.dot(total, poly, precision=highest)
        if iteration + 1 < NS_STEPS:
            square = jnp.dot(
                jnp.dot(poly, square, precision=highest), poly, precision=highest
            )
    return jnp.dot(gradient * inverse_norm, total, precision=highest)


def head_terms(inputs, weight, rate_weight, fast):
    head_dim = fast.shape[2]
    projected = jnp.dot(inputs, weight, preferred_element_type=jnp.float32)
    rates = jax.nn.softplus(
        jnp.dot(inputs, rate_weight[:, None], preferred_element_type=jnp.float32)
    )
    query_rows = unit_rows(swish(projected[:, :head_dim])).astype(jnp.bfloat16)
    key_rows = unit_rows(swish(projected[:, head_dim : 2 * head_dim])).astype(jnp.bfloat16)
    value_rows = projected[:, 2 * head_dim :].astype(jnp.bfloat16)
    gate_fast, up_fast, down_fast = fast[0], fast[1], fast[2]

    def dot_nt(a, b):
        return lax.dot_general(
            a, b, (((1,), (1,)), ((), ())), preferred_element_type=jnp.float32
        )

    gate_query = dot_nt(query_rows, gate_fast)
    up_query = dot_nt(query_rows, up_fast)
    hidden = (swish(gate_query) * up_query).astype(jnp.bfloat16)
    mixture = jnp.dot(hidden, down_fast, preferred_element_type=jnp.float32)
    head_out = (
        mixture * lax.rsqrt(jnp.mean(mixture * mixture, axis=-1, keepdims=True) + 1e-05)
    ).astype(jnp.bfloat16)
    gate_pre = dot_nt(key_rows, gate_fast)
    up_pre = dot_nt(key_rows, up_fast)
    sigma = jax.nn.sigmoid(gate_pre)
    gate_act = gate_pre * sigma
    key_hidden = (gate_act * up_pre).astype(jnp.bfloat16)
    scaled_values = (rates * value_rows.astype(jnp.float32)).astype(jnp.bfloat16)
    hidden_grad = -dot_nt(scaled_values, down_fast)
    up_grad = (hidden_grad * gate_act).astype(jnp.bfloat16)
    gate_grad = (hidden_grad * up_pre * sigma * (1.0 + gate_pre * (1.0 - sigma))).astype(
        jnp.bfloat16
    )
    update = jnp.stack(
        [
            orthogonalize(matmul_tn(gate_grad, key_rows)),
            orthogonalize(matmul_tn(up_grad, key_rows)),
            orthogonalize(-matmul_tn(key_hidden, scaled_values)),
        ]
    )
    return head_out, update.astype(jnp.bfloat16)


def local(fresh_input, carried, qkv_weight, out_weight, rate_weight, fast_state):
    received = from_behind(carried, "sec", 1)
    is_first = lax.axis_index("sec") == 0
    inputs = jnp.where(is_first, fresh_input[None], received)[0, 0]
    heads = rate_weight.shape[2]
    head_dim = fast_state.shape[5]
    depth = rate_weight.shape[1]
    previous = fast_state[0, 0]
    slots = head_slots(heads)
    each = slots // lax.axis_size("ctx")

    all_inputs = lax.all_gather(inputs, "ctx", axis=0, tiled=True)
    full_out = lax.all_gather(out_weight[0], ("ctx", "dp"), axis=0, tiled=True)
    full_rate = lax.all_gather(rate_weight[0], ("ctx", "dp"), axis=0, tiled=True)

    fast = exchange(pad_axis(previous.astype(jnp.bfloat16), 1, slots), 1, 2)
    columns = qkv_weight[0].reshape(depth, 3, heads, head_dim).transpose(2, 0, 1, 3)
    columns = columns.reshape(heads, depth, 3 * head_dim)
    columns = exchange(pad_axis(columns, 0, slots), 0, 1)
    columns = lax.all_gather(
        columns.reshape(each, lax.axis_size("ctx"), depth, 3 * head_dim), "dp", axis=2, tiled=True
    ).reshape(each, -1, 3 * head_dim)
    first = lax.axis_index("ctx") * each
    rate_columns = lax.dynamic_slice_in_dim(pad_axis(full_rate, 1, slots), first, each, 1)

    outs, updates = [], []
    for slot in range(each):
        head_out, update = head_terms(
            all_inputs, columns[slot], rate_columns[:, slot], fast[:, slot]
        )
        outs.append(head_out)
        updates.append(update)
    head_out = exchange(jnp.concatenate(outs, axis=1), 0, 1)[:, : heads * head_dim]
    branch_out = jnp.dot(head_out, full_out, preferred_element_type=jnp.float32)
    passed = (inputs.astype(jnp.float32) + branch_out).astype(jnp.bfloat16)

    update = exchange(jnp.stack(updates, axis=1), 2, 1)[:, :heads]
    stepped = previous - update_scale * update.astype(jnp.float32)
    rescale = jnp.sqrt(jnp.mean(previous * previous, axis=-1, keepdims=True) + 1e-06) * lax.rsqrt(
        jnp.mean(stepped * stepped, axis=-1, keepdims=True) + 1e-06
    )
    new_state = (stepped * rescale)[None, None]
    return (passed[None, None], new_state)


def solution(mesh):
    in_specs = (
        P("dp", "ctx", None),
        P("sec", "dp", "ctx", None),
        P("sec", ("ctx", "dp"), None),
        P("sec", ("ctx", "dp"), None),
        P("sec", ("ctx", "dp"), None),
        P("sec", "dp", None, None, "ctx", None),
    )
    out_specs = (P("sec", "dp", "ctx", None), P("sec", "dp", None, None, "ctx", None))
    return jax.shard_map(local, mesh=mesh, in_specs=in_specs, out_specs=out_specs, check_vma=False)
```

time: 688 us -> 338 us (0.49)
  waiting for transfers between devices: 524 us -> 61.6 us
  blocking collectives: 24 us -> 128 us
  starting transfers between devices: 3.93 us -> 22.4 us
  local copies, waits for them, and re-layouts: 24.2 us -> 11.8 us
    psum x2 -> x0, waiting for transfers between devices: 205 us -> none  [local(): lax.psum(gram_local(current).astype(jnp.bfloat16), 'ctx')]
    all_gather x3, waiting for transfers between devices: 190 us -> 13.8 us  [the longest x1 11.5 us: local(): lax.all_gather(columns.reshape(each, lax.axis_size('ctx'), depth, 3 * hea...]
    reduce_scatter x1 -> x0, waiting for transfers between devices: 128 us -> none  [local(): lax.psum_scatter(partial_value.astype(jnp.bfloat16), 'ctx', scatter_dimen...]
    all_to_all x0 -> x1, blocking collectives: none -> 55.7 us  [exchange(): lax.all_to_all(block, 'ctx', split_axis=split, concat_axis=concat, tiled=...]
    all_gather x1, blocking collectives: 24 us -> 71.8 us  [local(): lax.all_gather(rate_weight[0], ('ctx', 'dp'), axis=0, tiled=True)]
    all_to_all x0 -> x3, waiting for transfers between devices: none -> 30 us  [exchange(): lax.all_to_all(block, 'ctx', split_axis=split, concat_axis=concat, tiled=...]
    all_to_all x0 -> x3, starting transfers between devices: none -> 18.7 us  [exchange(): lax.all_to_all(block, 'ctx', split_axis=split, concat_axis=concat, tiled=...]
    dot_general x1 -> x0, local copies, waits for them, and re-layouts: 18.6 us -> none  [local(): projected = jnp.dot(inputs, full_qkv, preferred_element_type=jnp.float32)]
  transfers between devices with their start and end apart: 7 -> 7, of which waited for: 6 -> 4; matrix products, arithmetic and copies ran while one was open for 10% -> 29% of each run, Pallas kernels for 0% -> 0%
where the time goes in v1:
time: 338 us; the launch traced here: 331 us
  blocking collectives  128 us (38%)
  matrix products  83.4 us (25%)
  waiting for transfers between devices  61.6 us (18%)
  starting transfers between devices  22.4 us (7%)
  between operations  16.7 us (5%)
  local copies, waits for them, and re-layouts  11.8 us (3%)
  other arithmetic  7.84 us (2%)
    all_gather x1, blocking collectives, local(): lax.all_gather(rate_weight[0], ('ctx', 'dp'), axis=0, tiled=True)  71.8 us
    all_to_all x1, blocking collectives, exchange(): lax.all_to_all(block, 'ctx', split_axis=split, concat_axis=concat, tiled=...  55.7 us
    all_to_all x3, waiting for transfers between devices, exchange(): lax.all_to_all(block, 'ctx', split_axis=split, concat_axis=concat, tiled=...  30 us
    dot_general x6, matrix products, matmul_tn(): lax.dot_general(a, b, (((0,), (0,)), ((), ())), preferred_element_type=jn...  28 us
    all_to_all x3, starting transfers between devices, exchange(): lax.all_to_all(block, 'ctx', split_axis=split, concat_axis=concat, tiled=...  18.7 us
    ppermute x1, waiting for transfers between devices, from_behind(): return lax.ppermute(block, axis, route)  17 us
    dot_general x4, matrix products, dot_nt(): lax.dot_general(a, b, (((1,), (1,)), ((), ())), preferred_element_type=jn...  15 us
    all_gather x1, waiting for transfers between devices, local(): lax.all_gather(columns.reshape(each, lax.axis_size('ctx'), depth, 3 * hea...  11.5 us
  transfers between devices with their start and end apart: 7, of which 4 were waited for; matrix products, arithmetic and copies ran while one was open for 29% of the time, Pallas kernels for 0%

profile of v1, /device:TPU:24, one launch (start us, length us, event | category | flops | bytes accessed | tf_op | source)
XLA Modules:
  0.0 331.2 jit_solution(8719668244203159618)
XLA Ops:
  7.2 3.6 %collective-permute-start = (bf16[1,1,256,1536]{3,2,1,0:T(8,128)(2,1)}, bf16[1,1,256,1536]{3,2,1,0:T(8,128)(2,1)S(1)}, u32[]{:S(2)}, u32[]{:S(2)}) collective-permute-start(bf16[1,1,256,1536]{3,2,1,0:T(8,128)(2,1)} %param.7), channel_id=1, source_target_pairs={{0,2},{1,3},{4,6},{5,7},{8,10},{9,11},{12,14},{13,15},{16,18},{17,... | collective-permute-start | bytes 2359304 | tf_op jit(solution)/shard_map/ppermute | solution.py:19
  10.8 17.0 %collective-permute-done = bf16[1,1,256,1536]{3,2,1,0:T(8,128)(2,1)S(1)} collective-permute-done((bf16[1,1,256,1536]{3,2,1,0:T(8,128)(2,1)}, bf16[1,1,256,1536]{3,2,1,0:T(8,128)(2,1)S(1)}, u32[]{:S(2)}, u32[]{:S(2)}) %collective-permute-start) | collective-permute-done | bytes 786464 | tf_op jit(solution)/shard_map/ppermute | solution.py:19
  32.7 55.7 %all_to_all.49 = bf16[8,96,768]{2,1,0:T(8,128)(2,1)} all-to-all(bf16[8,96,768]{2,1,0:T(8,128)(2,1)S(1)} %pad.12), channel_id=1, replica_groups=mesh['ctx'=8,'sec'=2,'dp'=2] {'ctx'}, dimensions={0} | all-to-all | bytes 2359296 | tf_op jit(solution)/shard_map/all_to_all | solution.py:43
  89.7 6.7 %all-to-all-start.1 = ((bf16[3,8,96,256]{3,2,0,1:T(8,128)(2,1)}), bf16[3,8,96,256]{3,2,0,1:T(8,128)(2,1)S(1)}, u32[]{:S(2)}, u32[]{:S(2)}) async-start(bf16[3,8,96,256]{3,2,0,1:T(8,128)(2,1)} %pad.13.clone), calls=%async_computation.1 | async-start | bytes 2359296 | tf_op jit(solution)/shard_map/all_to_all | solution.py:43
  97.3 71.8 %all-gather.3 = bf16[1,1536,6]{2,0,1:T(2,128)(2,1)} all-gather(bf16[1,96,6]{2,0,1:T(2,128)(2,1)S(1)} %copy.26), channel_id=5, replica_groups=mesh['ctx'=8,'sec'=2,'dp'=2] {'ctx','dp'}, dimensions={1}, use_global_device_ids=true | all-gather | bytes 19584 | tf_op jit(solution)/shard_map/all_gather | solution.py:126
  172.4 2.3 all-gather.8.cloned.1.call-done
  174.7 4.5 %fusion = f32[1,2048]{1,0:T(1,128)S(1)} fusion(bf16[1,1,2048,1536]{3,2,1,0:T(8,128)(2,1)} %all-gather.8.cloned.1.call-done, s32[]{:T(128)S(6)} %select_n.29, bf16[1536,6]{0,1:T(8,128)(2,1)S(1)} %bitcast.94), kind=kOutput, calls=%fused_computation | convolution fusion | flops 6291456 | bytes 6318084 | tf_op jit(solution)/shard_map/dot_general | solution.py:73
  179.3 11.5 %all-gather.10.cloned.1.call-done = bf16[8,192,768]{2,1,0:T(8,128)(2,1)} async-done(((bf16[8,96,768]{2,1,0:T(8,128)(2,1)}), bf16[8,192,768]{2,1,0:T(8,128)(2,1)}) %all-gather.10.cloned.1.call-update) | async-done | bytes 2359312 | tf_op jit(solution)/shard_map/all_gather | solution.py:132
  190.7 8.1 %fusion.2 = f32[2048,768]{0,1:T(8,128)S(1)} fusion(bf16[1536,768]{1,0:T(8,128)(2,1)} %bitcast.96, bf16[1,1,2048,1536]{3,2,1,0:T(8,128)(2,1)} %all-gather.8.cloned.1.call-done), kind=kOutput, calls=%fused_computation.2 | convolution fusion | flops 4831838208 | bytes 14942208 | tf_op jit(solution)/shard_map/dot_general | solution.py:71
  200.2 4.1 %fusion.50 = f32[2048,768]{1,0:T(8,128)} fusion(bf16[768,256]{1,0:T(8,128)(2,1)S(1)} %bitcast.92, f32[2048]{0:T(1024)S(1)} %add_sqrt_fusion, f32[2048,768]{0,1:T(8,128)S(1)} %fusion.2), kind=kOutput, calls=%fused_computation.99 | convolution fusion | flops 808452096 | bytes 8790016 | tf_op jit(solution)/shard_map/dot_general | solution.py:81
  204.3 4.1 %fusion.49 = f32[2048,768]{1,0:T(8,128)} fusion(bf16[768,256]{1,0:T(8,128)(2,1)S(1)} %bitcast.93, f32[2048]{0:T(1024)S(1)} %add_sqrt_fusion.1, f32[2048,768]{0,1:T(8,128)S(1)} %fusion.2), kind=kOutput, calls=%fused_computation.98 | convolution fusion | flops 808452096 | bytes 8790016 | tf_op jit(solution)/shard_map/dot_general | solution.py:81
  208.4 4.1 %fusion.51 = f32[2048,768]{1,0:T(8,128)} fusion(bf16[768,256]{1,0:T(8,128)(2,1)S(1)} %bitcast.90, f32[2048]{0:T(1024)S(1)} %add_sqrt_fusion, f32[2048,768]{0,1:T(8,128)S(1)} %fusion.2), kind=kOutput, calls=%fused_computation.100 | convolution fusion | flops 808452096 | bytes 8790016 | tf_op jit(solution)/shard_map/dot_general | solution.py:81
  212.4 7.3 %multiply_reduce_fusion.1 = (f32[2048]{0:T(1024)S(1)}, f32[2048,256]{1,0:T(8,128)}) fusion(bf16[768,256]{1,0:T(8,128)(2,1)S(1)} %bitcast.88, f32[2048,768]{1,0:T(8,128)} %fusion.49, bf16[768,256]{1,0:T(8,128)(2,1)S(1)} %bitcast.91, f32[2048]{0:T(1024)S(1)} %add_sqrt_fusion.1, f32[2048,768]{0,1:T(8,128)} %copy-done.3), kind=kOutput, calls=%fused_computation.21 | convolution fusion | flops 1624242176 | bytes 11288576 | tf_op jit(solution)/shard_map/dot_general | solution.py:88
  223.0 6.2 %all-to-all-start.2 = ((bf16[8,256,256]{1,2,0:T(8,128)(2,1)}), bf16[8,256,256]{1,2,0:T(8,128)(2,1)}, u32[]{:S(2)}, u32[]{:S(2)}) async-start(bf16[8,256,256]{1,2,0:T(8,128)(2,1)} %copy.25), calls=%async_computation.2 | async-start | bytes 2097152 | tf_op jit(solution)/shard_map/all_to_all | solution.py:43
  229.2 2.8 fusion.33
  232.0 8.5 %fusion.7 = f32[768,256]{1,0:T(8,128)S(1)} fusion(f32[2048,768]{1,0:T(8,128)S(1)} %fusion.33, f32[2048,768]{1,0:T(8,128)} %fusion.50, f32[2048]{0:T(1024)S(1)} %add_sqrt_fusion, f32[2048,768]{0,1:T(8,128)} %copy-done.3), kind=kOutput, calls=%fused_computation.12 | convolution fusion | flops 819462144 | bytes 15474688 | tf_op jit(solution)/shard_map/dot_general | solution.py:47
  240.6 3.7 %fusion.13 = f32[768,256]{1,0:T(8,128)S(1)} fusion(f32[2048,768]{1,0:T(8,128)S(1)} %bitcast.100, f32[2048,768]{1,0:T(8,128)S(1)} %bitcast.98, f32[2048,768]{0,1:T(8,128)} %copy-done.3, f32[2048]{0:T(1024)S(1)} %compare_select_fusion), kind=kOutput, calls=%fused_computation.34 | convolution fusion | flops 816513024 | bytes 14426112 | tf_op jit(solution)/shard_map/dot_general | solution.py:47
  244.2 2.8 select_reduce_fusion
  247.7 2.7 select_reduce_fusion.1
  259.3 7.6 %fusion.9 = f32[768,256]{1,0:T(8,128)S(1)} fusion(f32[2048,768]{1,0:T(8,128)} %fusion.50, f32[2048,768]{1,0:T(8,128)} %fusion.51, f32[2048,768]{1,0:T(8,128)S(1)} %copy-done.1, f32[2048]{0:T(1024)S(1)} %add_sqrt_fusion, f32[2048,768]{0,1:T(8,128)} %copy-done.3), kind=kOutput, calls=%fused_computation.14 | convolution fusion | flops 825753600 | bytes 21766144 | tf_op jit(solution)/shard_map/dot_general | solution.py:47
  267.7 2.8 select_reduce_fusion.2
  280.9 5.8 %all-to-all-start.3 = ((bf16[3,1,768,256]{3,0,1,2:T(4,128)(2,1)}), bf16[3,1,768,256]{3,0,1,2:T(4,128)(2,1)S(1)}, u32[]{:S(2)}, u32[]{:S(2)}) async-start(bf16[3,1,768,256]{3,0,1,2:T(4,128)(2,1)} %copy.28), calls=%async_computation.3 | async-start | bytes 3145728 | tf_op jit(solution)/shard_map/all_to_all | solution.py:43
  286.7 5.1 %fusion.25 = bf16[1,1,256,1536]{3,2,1,0:T(8,128)(2,1)} fusion(bf16[1,1,256,1536]{3,2,1,0:T(8,128)(2,1)} %bitcast_select_fusion, bf16[1,1536,1536]{2,1,0:T(8,128)(2,1)} %all-gather.12.cloned.1.call-done, bf16[256,2048]{0,1:T(8,128)(2,1)} %bitcast.11), kind=kOutput, calls=%fused_computation.54 | convolution fusion | flops 1209139200 | bytes 7077888 | tf_op jit(solution)/shard_map/dot_general | solution.py:146
  291.8 30.0 %all-to-all-done.3 = bf16[3,1,768,256]{3,0,1,2:T(4,128)(2,1)S(1)} async-done(((bf16[3,1,768,256]{3,0,1,2:T(4,128)(2,1)}), bf16[3,1,768,256]{3,0,1,2:T(4,128)(2,1)S(1)}, u32[]{:S(2)}, u32[]{:S(2)}) %all-to-all-start.3) | async-done | bytes 1179680 | tf_op jit(solution)/shard_map/all_to_all | solution.py:43
  (85 shorter events, 35.8 us)
Async XLA Ops:
  7.2 22.9 %copy-start.8 = (bf16[1,96,4608]{2,1,0:T(8,128)(2,1)S(1)}, bf16[1,96,4608]{2,1,0:T(8,128)(2,1)}, u32[]{:S(2)}) copy-start(bf16[1,96,4608]{2,1,0:T(8,128)(2,1)} %param.8) | copy-start | bytes 2654212
  7.2 167.6 %all-gather.8.cloned.1.call-start = ((), (), s32[]{:S(2)}) async-start(), calls=%async_computation.4 | async-start | bytes 7077888 | tf_op jit(solution)/shard_map/all_gather | solution.py:124
  7.2 20.7 %collective-permute-start = (bf16[1,1,256,1536]{3,2,1,0:T(8,128)(2,1)}, bf16[1,1,256,1536]{3,2,1,0:T(8,128)(2,1)S(1)}, u32[]{:S(2)}, u32[]{:S(2)}) collective-permute-start(bf16[1,1,256,1536]{3,2,1,0:T(8,128)(2,1)} %param.7), channel_id=1, source_target_pairs={{0,2},{1,3},{4,6},{5,7},{8,10},{9,11},{12,14},{13,15},{16,18},{17,... | collective-permute-start | bytes 2359304 | tf_op jit(solution)/shard_map/ppermute | solution.py:19
  30.0 160.7 %all-gather.10.cloned.1.call-start = ((), (), s32[]{:S(2)}) async-start(), calls=%async_computation.5 | async-start | bytes 3538944 | tf_op jit(solution)/shard_map/all_gather | solution.py:132
  32.7 55.7 %copy-start.2 = (f32[1,1,3,6,96,256]{5,4,3,2,1,0:T(8,128)S(1)}, f32[1,1,3,6,96,256]{5,4,3,2,1,0:T(8,128)}, u32[]{:S(2)}) copy-start(f32[1,1,3,6,96,256]{5,4,3,2,1,0:T(8,128)} %param.11) | copy-start | bytes 5308420
  88.6 8.5 %copy-start.11 = (bf16[1,96,6]{1,2,0:T(8,128)(2,1)S(1)}, bf16[1,96,6]{1,2,0:T(8,128)(2,1)}, u32[]{:S(2)}) copy-start(bf16[1,96,6]{1,2,0:T(8,128)(2,1)} %param.10) | copy-start | bytes 3460
  89.7 81.7 %all-to-all-start.1 = ((bf16[3,8,96,256]{3,2,0,1:T(8,128)(2,1)}), bf16[3,8,96,256]{3,2,0,1:T(8,128)(2,1)S(1)}, u32[]{:S(2)}, u32[]{:S(2)}) async-start(bf16[3,8,96,256]{3,2,0,1:T(8,128)(2,1)} %pad.13.clone), calls=%async_computation.1 | async-start | bytes 2359296 | tf_op jit(solution)/shard_map/all_to_all | solution.py:43
  96.4 190.3 %all-gather.12.cloned.1.call-start = ((), (), s32[]{:S(2)}) async-start(), calls=%async_computation.6 | async-start | bytes 5013504 | tf_op jit(solution)/shard_map/all_gather | solution.py:125
  198.8 9.5 %copy-start.3 = (f32[2048,768]{0,1:T(8,128)}, f32[2048,768]{0,1:T(8,128)S(1)}, u32[]{:S(2)}) copy-start(f32[2048,768]{0,1:T(8,128)S(1)} %fusion.2) | copy-start | bytes 18874372
  198.9 1.3 copy-start.10
  204.3 4.1 %copy-start.9 = (bf16[1,8,96,256]{3,2,0,1:T(8,128)(2,1)S(1)}, bf16[1,8,96,256]{3,2,0,1:T(8,128)(2,1)}, u32[]{:S(2)}) copy-start(bf16[1,8,96,256]{3,2,0,1:T(8,128)(2,1)} %get-tuple-element.8) | copy-start | bytes 1179652
  223.0 57.9 %all-to-all-start.2 = ((bf16[8,256,256]{1,2,0:T(8,128)(2,1)}), bf16[8,256,256]{1,2,0:T(8,128)(2,1)}, u32[]{:S(2)}, u32[]{:S(2)}) async-start(bf16[8,256,256]{1,2,0:T(8,128)(2,1)} %copy.25), calls=%async_computation.2 | async-start | bytes 2097152 | tf_op jit(solution)/shard_map/all_to_all | solution.py:43
  229.2 11.4 %slice-start = ((s8[6291456]{0:T(1024)(128)(4,1)}), s8[4194304]{0:T(1024)(128)(4,1)S(1)}, s32[]{:S(2)}) async-start(s8[6291456]{0:T(1024)(128)(4,1)} %bitcast.97), calls=%async_computation.7 | async-start | bytes 8388608
  229.2 11.4 %slice-start.2 = ((s8[6291456]{0:T(1024)(128)(4,1)}), s8[4194304]{0:T(1024)(128)(4,1)S(1)}, s32[]{:S(2)}) async-start(s8[6291456]{0:T(1024)(128)(4,1)} %bitcast.99), calls=%async_computation.9 | async-start | bytes 8388608
  232.0 8.6 %copy-start = (f32[2048,768]{1,0:T(8,128)}, f32[2048,768]{1,0:T(8,128)S(1)}, u32[]{:S(2)}) copy-start(f32[2048,768]{1,0:T(8,128)S(1)} %fusion.33) | copy-start | bytes 18874372
  232.0 8.6 %slice-start.1 = ((s8[6291456]{0:T(1024)(128)(4,1)}), s8[2097152]{0:T(1024)(128)(4,1)S(1)}, s32[]{:S(2)}) async-start(s8[6291456]{0:T(1024)(128)(4,1)} %bitcast.97), calls=%async_computation.8 | async-start | bytes 4194304
  232.0 8.6 %slice-start.3 = ((s8[6291456]{0:T(1024)(128)(4,1)}), s8[2097152]{0:T(1024)(128)(4,1)S(1)}, s32[]{:S(2)}) async-start(s8[6291456]{0:T(1024)(128)(4,1)} %bitcast.99), calls=%async_computation.10 | async-start | bytes 4194304
  251.1 7.0 %copy-start.7 = (f32[256,256]{1,0:T(8,128)S(1)}, f32[256,256]{1,0:T(8,128)}, u32[]{:S(2)}) copy-start(f32[256,256]{1,0:T(8,128)} %get-tuple-element.16) | copy-start | bytes 786436
  251.1 8.1 %copy-start.1 = (f32[2048,768]{1,0:T(8,128)S(1)}, f32[2048,768]{1,0:T(8,128)}, u32[]{:S(2)}) copy-start(f32[2048,768]{1,0:T(8,128)} %copy-done) | copy-start | bytes 18874372
  266.8 0.9 copy-start.4
  272.2 3.6 %copy-start.6 = (f32[256,256]{1,0:T(8,128)S(1)}, f32[256,256]{1,0:T(8,128)}, u32[]{:S(2)}) copy-start(f32[256,256]{1,0:T(8,128)} %get-tuple-element.18) | copy-start | bytes 786436
  275.8 2.0 copy-start.5
  280.9 40.9 %all-to-all-start.3 = ((bf16[3,1,768,256]{3,0,1,2:T(4,128)(2,1)}), bf16[3,1,768,256]{3,0,1,2:T(4,128)(2,1)S(1)}, u32[]{:S(2)}, u32[]{:S(2)}) async-start(bf16[3,1,768,256]{3,0,1,2:T(4,128)(2,1)} %copy.28), calls=%async_computation.3 | async-start | bytes 3145728 | tf_op jit(solution)/shard_map/all_to_all | solution.py:43
Sparse Core Ops, SparseCore 0:
  30.1 144.5 all-gather.7
  176.3 14.3 all-gather.9
  193.0 67.1 all-gather.11

commit v2 on v1

v2 whole, which is shorter than its diff:
```python
import functools

import jax
import jax.numpy as jnp
from jax import lax
from jax.experimental import pallas as pl
from jax.experimental.pallas import tpu as pltpu
from jax.sharding import PartitionSpec as P

NS_STEPS = 2
LANES = 128
PAIR = 2
VMEM_BYTES = 56 * 2**20

linear_coef = 3.4445
cubic_coef = -4.775
quintic_coef = 2.0315
update_scale = 8.0
highest = lax.Precision.HIGHEST
MESH = pl.DeviceIdType.MESH


def swish(values):
    return values * jax.nn.sigmoid(values)


def unit_rows(values):
    return values * lax.rsqrt(jnp.sum(values * values, axis=-1, keepdims=True) + 1e-06)


def dot_nn(a, b, precision=None):
    return jnp.dot(a, b, preferred_element_type=jnp.float32, precision=precision)


def dot_nt(a, b):
    return lax.dot_general(a, b, (((1,), (1,)), ((), ())), preferred_element_type=jnp.float32)


def dot_tn(a, b, precision=None):
    return lax.dot_general(
        a, b, (((0,), (0,)), ((), ())), preferred_element_type=jnp.float32, precision=precision
    )


def orthogonalize(gradient):
    square = dot_tn(gradient, gradient, highest)
    rows = lax.broadcasted_iota(jnp.int32, square.shape, 0)
    columns = lax.broadcasted_iota(jnp.int32, square.shape, 1)
    eye = (rows == columns).astype(jnp.float32)
    trace = jnp.sum(jnp.sum(square * eye, axis=1, keepdims=True), axis=0, keepdims=True)
    inverse_norm = lax.rsqrt(trace + 1e-06)
    square = square * inverse_norm * inverse_norm
    total = None
    for iteration in range(NS_STEPS):
        quad = dot_nn(square, square, highest)
        poly = linear_coef * eye + cubic_coef * square + quintic_coef * quad
        total = poly if total is None else dot_nn(total, poly, highest)
        if iteration + 1 < NS_STEPS:
            square = dot_nn(dot_nn(poly, square, highest), poly, highest)
    return dot_nn(gradient * inverse_norm, total, highest)


def block_terms(inputs, weight_ref, fast_ref, gradient_ref):
    head_dim = fast_ref.shape[2]
    weight = weight_ref[...].reshape(inputs.shape[1], weight_ref.shape[3])
    projected = dot_nn(inputs, weight)
    query_rows = unit_rows(swish(projected[:, :head_dim])).astype(jnp.bfloat16)
    key_rows = unit_rows(swish(projected[:, head_dim : 2 * head_dim])).astype(jnp.bfloat16)
    value_rows = projected[:, 2 * head_dim : 3 * head_dim].astype(jnp.bfloat16)
    rates = jax.nn.softplus(projected[:, 3 * head_dim : 3 * head_dim + 1])
    scaled_values = (rates * value_rows.astype(jnp.float32)).astype(jnp.bfloat16)

    gate_query = dot_nt(query_rows, fast_ref[0])
    up_query = dot_nt(query_rows, fast_ref[1])
    hidden = (swish(gate_query) * up_query).astype(jnp.bfloat16)
    mixture = dot_nn(hidden, fast_ref[2])
    head_out = mixture * lax.rsqrt(jnp.mean(mixture * mixture, axis=-1, keepdims=True) + 1e-05)

    gate_pre = dot_nt(key_rows, fast_ref[0])
    up_pre = dot_nt(key_rows, fast_ref[1])
    sigma = jax.nn.sigmoid(gate_pre)
    gate_act = gate_pre * sigma
    key_hidden = (gate_act * up_pre).astype(jnp.bfloat16)
    hidden_grad = -dot_nt(scaled_values, fast_ref[2])
    up_grad = (hidden_grad * gate_act).astype(jnp.bfloat16)
    gate_grad = (hidden_grad * up_pre * sigma * (1.0 + gate_pre * (1.0 - sigma))).astype(
        jnp.bfloat16
    )
    gradient_ref[0] += dot_tn(gate_grad, key_rows)
    gradient_ref[1] += dot_tn(up_grad, key_rows)
    gradient_ref[2] -= dot_tn(key_hidden, scaled_values)
    return head_out.astype(jnp.bfloat16)


def kernel(
    sizes, fresh, carried, columns, fast_rows, inputs_out, head_out, update_out,
    blocks, weight, fast, gradient, out_stage, out_land, update_stage, update_land,
    y_sem, load_sem, own_sem, w_send, w_recv, f_send, f_recv, d_send, d_recv,
    up_send, down_send, line_recv, pair_send, pair_recv, h_send, h_recv, u_send, u_recv,
):
    n_ctx, n_sec, n_dp, heads = sizes
    lines = n_ctx // PAIR
    me = lax.axis_index("ctx")
    sec = lax.axis_index("sec")
    dp = lax.axis_index("dp")
    line, side = me // PAIR, lax.rem(me, PAIR)
    hidden_rows = fast_rows.shape[2]
    head_dim = fast_rows.shape[3]
    owner = me < heads
    from_sec = sec > 0
    to_sec = sec + 1 < n_sec

    def remote(src, dst, send, recv, **device):
        return pltpu.make_async_remote_copy(
            src_ref=src, dst_ref=dst, send_sem=send, recv_sem=recv,
            device_id=device, device_id_type=MESH,
        )

    def peer(step):
        return lax.rem(me + step, n_ctx)

    barrier = pltpu.get_barrier_semaphore()
    for step in range(1, n_ctx):
        pl.semaphore_signal(barrier, inc=1, device_id={"ctx": peer(step)}, device_id_type=MESH)
    for step in range(1, n_dp):
        pl.semaphore_signal(
            barrier, inc=1, device_id={"dp": lax.rem(dp + step, n_dp)}, device_id_type=MESH
        )

    for step in range(1, n_sec):
        pl.semaphore_signal(
            barrier, inc=1, device_id={"sec": lax.rem(sec + step, n_sec)}, device_id_type=MESH
        )
    pl.semaphore_wait(barrier, n_ctx + n_dp + n_sec - 3)

    def y_copy():
        return remote(
            carried.at[0, 0], blocks.at[me], y_sem.at[0], y_sem.at[1], sec=lax.rem(sec + 1, n_sec)
        )

    def fresh_copy():
        return pltpu.make_async_copy(fresh.at[0], blocks.at[me], load_sem)

    @pl.when(to_sec)
    def _():
        y_copy().start()

    @pl.when(sec == 0)
    def _():
        fresh_copy().start()

    my_rows = pl.ds(pl.multiple_of(me * hidden_rows, hidden_rows), hidden_rows)

    def w_copy(target):
        return remote(
            columns.at[target], weight.at[me, dp], w_send.at[target], w_recv.at[me], ctx=target
        )

    def f_copy(target):
        return remote(
            fast_rows.at[:, target], fast.at[:, my_rows], f_send.at[target], f_recv.at[me],
            ctx=target,
        )

    def own_copies():
        return (
            pltpu.make_async_copy(columns.at[me], weight.at[me, dp], own_sem.at[0]),
            pltpu.make_async_copy(fast_rows.at[:, me], fast.at[:, my_rows], own_sem.at[1]),
        )

    for step in range(1, n_ctx):
        target = peer(step)

        @pl.when(target < heads)
        def _():
            w_copy(target).start()

    for step in range(1, n_ctx):
        target = peer(step)

        @pl.when(target < heads)
        def _():
            f_copy(target).start()

    @pl.when(owner)
    def _():
        for copy in own_copies():
            copy.start()
        gradient[...] = jnp.zeros_like(gradient)

    def shard(row, which):
        return row * PAIR + which

    def line_copy(row, sem, to_line):
        at = shard(row, side)
        return remote(
            blocks.at[at], blocks.at[at], sem.at[row], line_recv.at[row],
            ctx=shard(to_line, side),
        )

    def pair_copy(row):
        at = shard(row, side)
        return remote(
            blocks.at[at], blocks.at[at], pair_send.at[row], pair_recv.at[row],
            ctx=shard(line, 1 - side),
        )

    def pass_on(row, distance, sign):
        @pl.when(distance > 0)
        def _():
            remote(
                blocks.at[shard(row, side)], blocks.at[shard(row, side)],
                up_send.at[row], line_recv.at[row], ctx=peer(1),
            ).wait_recv()

        @pl.when((row <= line) & (line + 1 < lines))
        def _():
            line_copy(row, up_send, line + 1).start()

        @pl.when((row >= line) & (line > 0))
        def _():
            line_copy(row, down_send, line - 1).start()

        pair_copy(row).start()

    def out_copy(at):
        return remote(
            out_stage.at[at], out_land.at[me], h_send.at[at], h_recv.at[me], ctx=at
        )

    def compute(at):
        out = block_terms(blocks[at], weight, fast, gradient)

        @pl.when(at == me)
        def _():
            out_land[me] = out

        @pl.when(at != me)
        def _():
            out_stage[at] = out
            out_copy(at).start()

    def rows_at(distance, sign):
        row = line + distance * (1 - 2 * sign)
        valid = (row >= 0) & (row < lines) & ((distance > 0) | (sign == 0))
        return row, valid

    @pl.when(sec == 0)
    def _():
        fresh_copy().wait()

    @pl.when(from_sec)
    def _():
        y_copy().wait_recv()

    def weights_ready():
        @pl.when(owner)
        def _():
            for step in range(1, n_ctx):
                source = peer(step)
                remote(
                    columns.at[0], weight.at[source, dp], w_send.at[0], w_recv.at[source],
                    ctx=source,
                ).wait_recv()
            for copy in own_copies():
                copy.wait()
            for step in range(1, n_dp):
                remote(
                    weight.at[:, dp], weight.at[:, dp], d_send.at[step], d_recv.at[step],
                    dp=lax.rem(dp + step, n_dp),
                ).start()
            for step in range(1, n_ctx):
                source = peer(step)
                rows = pl.ds(pl.multiple_of(source * hidden_rows, hidden_rows), hidden_rows)
                remote(
                    fast_rows.at[:, 0], fast.at[:, rows], f_send.at[0], f_recv.at[source],
                    ctx=source,
                ).wait_recv()
            for step in range(1, n_dp):
                source = lax.rem(dp + n_dp - step, n_dp)
                remote(
                    weight.at[:, source], weight.at[:, source], d_send.at[step], d_recv.at[step],
                    dp=source,
                ).wait()

    def step_body(distance, carry):
        @pl.when(distance < lines)
        def _():
            for sign in range(2):
                row, valid = rows_at(distance, sign)

                @pl.when(valid)
                def _():
                    pass_on(row, distance, sign)

        @pl.when(distance == 1)
        def _():
            weights_ready()

        @pl.when(distance > 0)
        def _():
            def block_body(index, inner):
                sign, far = index // 2, lax.rem(index, 2)
                row, valid = rows_at(distance - 1, sign)

                @pl.when(valid)
                def _():
                    at = shard(row, lax.rem(side + far, 2))

                    @pl.when(far == 1)
                    def _():
                        remote(
                            blocks.at[at], blocks.at[at], pair_send.at[row], pair_recv.at[row],
                            ctx=shard(line, 1 - side),
                        ).wait_recv()

                    @pl.when(owner)
                    def _():
                        compute(at)

                return inner

            lax.fori_loop(0, 4, block_body, 0)

        return carry

    lax.fori_loop(0, lines + 1, step_body, 0)

    def update_copy(target):
        rows = pl.ds(pl.multiple_of(target * hidden_rows, hidden_rows), hidden_rows)
        return remote(
            update_stage.at[:, rows], update_land.at[:, me], u_send.at[target], u_recv.at[me],
            ctx=target,
        )

    @pl.when(owner)
    def _():
        def matrix_body(which, carry):
            update_stage[which] = orthogonalize(gradient[which]).astype(jnp.bfloat16)
            return carry

        lax.fori_loop(0, 3, matrix_body, 0)
        for step in range(1, n_ctx):
            update_copy(peer(step)).start()
        update_land[:, me] = update_stage[:, my_rows]

    inputs_out[...] = blocks[me]
    for head in range(heads):
        @pl.when(me != head)
        def _():
            remote(
                out_stage.at[0], out_land.at[head], h_send.at[0], h_recv.at[head], ctx=head
            ).wait_recv()

        head_out[:, head * head_dim : (head + 1) * head_dim] = out_land[head]
    for head in range(heads):
        @pl.when(me != head)
        def _():
            remote(
                update_stage.at[:, pl.ds(0, hidden_rows)], update_land.at[:, head],
                u_send.at[0], u_recv.at[head], ctx=head,
            ).wait_recv()

    update_out[...] = update_land[:, :heads]

    @pl.when(to_sec)
    def _():
        y_copy().wait_send()

    for step in range(1, n_ctx):
        target = peer(step)

        @pl.when(target < heads)
        def _():
            w_copy(target).wait_send()
            f_copy(target).wait_send()

        @pl.when(owner)
        def _():
            out_copy(target).wait_send()
            update_copy(target).wait_send()

    for row in range(lines):
        @pl.when((row <= line) & (line + 1 < lines))
        def _():
            line_copy(row, up_send, lax.rem(line + 1, lines)).wait_send()

        @pl.when((row >= line) & (line > 0))
        def _():
            line_copy(row, down_send, lax.rem(line + lines - 1, lines)).wait_send()

        pair_copy(row).wait_send()


def local(fresh_input, carried, qkv_weight, out_weight, rate_weight, fast_state):
    n_ctx, n_sec, n_dp = (lax.axis_size(axis) for axis in ("ctx", "sec", "dp"))
    heads = rate_weight.shape[2]
    head_dim = fast_state.shape[5]
    hidden_rows = fast_state.shape[4]
    depth = rate_weight.shape[1]
    count, width = fresh_input.shape[1:]
    assert heads <= n_ctx and n_ctx % PAIR == 0
    previous = fast_state[0, 0]
    full_out = lax.all_gather(out_weight[0], ("ctx", "dp"), axis=0, tiled=True)

    columns = qkv_weight[0].reshape(depth, 3, heads, head_dim).transpose(2, 0, 1, 3)
    columns = columns.reshape(heads, depth, 3 * head_dim)
    rate_columns = jnp.pad(rate_weight[0].T[:, :, None], ((0, 0), (0, 0), (0, LANES - 1)))
    columns = jnp.concatenate([columns, rate_columns], axis=2)
    fast_rows = previous.astype(jnp.bfloat16)

    half = jnp.bfloat16
    dma = pltpu.SemaphoreType.DMA
    lines = n_ctx // PAIR
    any_spec = pl.BlockSpec(memory_space=pl.ANY)
    vmem_spec = pl.BlockSpec(memory_space=pltpu.VMEM)
    tokens = n_ctx * count
    hidden_all = n_ctx * hidden_rows
    flops = 2 * tokens * head_dim * (3 * width + 9 * hidden_all)
    inputs, head_out, update = pl.pallas_call(
        functools.partial(kernel, (n_ctx, n_sec, n_dp, heads)),
        out_shape=[
            jax.ShapeDtypeStruct((count, width), half),
            jax.ShapeDtypeStruct((count, heads * head_dim), half),
            jax.ShapeDtypeStruct((3, heads, hidden_rows, head_dim), half),
        ],
        in_specs=[any_spec] * 4,
        out_specs=[vmem_spec] * 3,
        scratch_shapes=[
            pltpu.VMEM((n_ctx, count, width), half),
            pltpu.VMEM((n_ctx, n_dp, depth, 3 * head_dim + LANES), half),
            pltpu.VMEM((3, hidden_all, head_dim), half),
            pltpu.VMEM((3, hidden_all, head_dim), jnp.float32),
            pltpu.VMEM((n_ctx, count, head_dim), half),
            pltpu.VMEM((n_ctx, count, head_dim), half),
            pltpu.VMEM((3, hidden_all, head_dim), half),
            pltpu.VMEM((3, n_ctx, hidden_rows, head_dim), half),
            dma((2,)), dma, dma((2,)),
            dma((n_ctx,)), dma((n_ctx,)), dma((n_ctx,)), dma((n_ctx,)),
            dma((n_dp,)), dma((n_dp,)),
            dma((lines,)), dma((lines,)), dma((lines,)), dma((lines,)), dma((lines,)),
            dma((n_ctx,)), dma((n_ctx,)), dma((n_ctx,)), dma((n_ctx,)),
        ],
        compiler_params=pltpu.CompilerParams(
            collective_id=0, has_side_effects=True, vmem_limit_bytes=VMEM_BYTES
        ),
        cost_estimate=pl.CostEstimate(
            flops=flops, bytes_accessed=tokens * width * 2, transcendentals=4 * tokens * hidden_all
        ),
    )(fresh_input, carried, columns, fast_rows)

    branch_out = jnp.dot(head_out, full_out, preferred_element_type=jnp.float32)
    passed = (inputs.astype(jnp.float32) + branch_out).astype(jnp.bfloat16)
    stepped = previous - update_scale * update.astype(jnp.float32)
    rescale = jnp.sqrt(jnp.mean(previous * previous, axis=-1, keepdims=True) + 1e-06) * lax.rsqrt(
        jnp.mean(stepped * stepped, axis=-1, keepdims=True) + 1e-06
    )
    new_state = (stepped * rescale)[None, None]
    return (passed[None, None], new_state)


def solution(mesh):
    in_specs = (
        P("dp", "ctx", None),
        P("sec", "dp", "ctx", None),
        P("sec", ("ctx", "dp"), None),
        P("sec", ("ctx", "dp"), None),
        P("sec", ("ctx", "dp"), None),
        P("sec", "dp", None, None, "ctx", None),
    )
    out_specs = (P("sec", "dp", "ctx", None), P("sec", "dp", None, None, "ctx", None))
    return jax.shard_map(local, mesh=mesh, in_specs=in_specs, out_specs=out_specs, check_vma=False)
```

time: 338 us -> 243 us (0.72); the launches traced: 331 us -> 241 us
  Pallas kernels: 0 us -> 210 us
  blocking collectives: 128 us -> 0 us
  matrix products: 83.4 us -> 4.6 us
  waiting for transfers between devices: 61.6 us -> 0.68 us
  starting transfers between devices: 22.4 us -> 0.04 us
  local copies, waits for them, and re-layouts: 11.8 us -> 5.65 us
    pallas_call x0 -> x1, Pallas kernels: none -> 210 us  [local(): pl.pallas_call(functools.partial(kernel, (n_ctx, n_sec, n_dp, heads)), ou...]
    dot_general x31 -> x0, matrix products: 78.3 us -> none  [the longest x6 28 us: matmul_tn(): lax.dot_general(a, b, (((0,), (0,)), ((), ())), preferred_element_type=jn...]
    all_gather x1 -> x0, blocking collectives: 71.8 us -> none  [local(): lax.all_gather(rate_weight[0], ('ctx', 'dp'), axis=0, tiled=True)]
    all_to_all x1 -> x0, blocking collectives: 55.7 us -> none  [exchange(): lax.all_to_all(block, 'ctx', split_axis=split, concat_axis=concat, tiled=...]
    all_to_all x3 -> x0, waiting for transfers between devices: 30 us -> none  [exchange(): lax.all_to_all(block, 'ctx', split_axis=split, concat_axis=concat, tiled=...]
    all_to_all x3 -> x0, starting transfers between devices: 18.7 us -> none  [exchange(): lax.all_to_all(block, 'ctx', split_axis=split, concat_axis=concat, tiled=...]
    ppermute x1 -> x0, waiting for transfers between devices: 17 us -> none  [from_behind(): return lax.ppermute(block, axis, route)]
    all_gather x2 -> x0, waiting for transfers between devices: 13.8 us -> none  [the longest x1 11.5 us: local(): lax.all_gather(columns.reshape(each, lax.axis_size('ctx'), depth, 3 * hea...]
  transfers between devices with their start and end apart: 7 -> 1, of which waited for: 4 -> 0; matrix products, arithmetic and copies ran while one was open for 29% -> 5% of each run, Pallas kernels for 0% -> 87%
where the time goes in v2:
time: 243 us; the launch traced here: 241 us
  Pallas kernels  210 us (86%)
  between operations  14.1 us (6%)
  other arithmetic  6.76 us (3%)
  local copies, waits for them, and re-layouts  5.65 us (2%)
  matrix products  4.6 us (2%)
    pallas_call x1, Pallas kernels, local(): pl.pallas_call(functools.partial(kernel, (n_ctx, n_sec, n_dp, heads)), ou...  210 us
  transfers between devices with their start and end apart: 1, of which 0 were waited for; matrix products, arithmetic and copies ran while one was open for 5% of the time, Pallas kernels for 87%

profile of v2, /device:TPU:24, one launch (start us, length us, event | category | flops | bytes accessed | tf_op | source)
XLA Modules:
  0.0 241.4 jit_solution(1742365984976462562)
XLA Ops:
  7.2 0.0 all-gather.3.cloned.1.call-start
  7.2 0.7 all-gather.3.cloned.1.call-update
  7.9 0.8 copy.10
  8.7 2.1 reshape_squeeze.3
  10.9 0.5 copy.9
  11.3 0.0 copy-start
  11.3 2.1 reshape.25
  13.5 2.2 fusion.13.columns
  15.7 0.0 copy-done
  15.7 1.1 bitcast_convert_fusion.fast_rows
  16.8 209.6 %shard_map.77 = (bf16[256,1536]{1,0:T(8,128)(2,1)}, bf16[256,1536]{1,0:T(8,128)(2,1)}, bf16[3,6,96,256]{3,2,1,0:T(8,128)(2,1)}) custom-call(bf16[1,256,1536]{2,1,0:T(8,128)(2,1)} %fresh.1, bf16[1,1,256,1536]{3,2,1,0:T(8,128)(2,1)} %carried.1, bf16[6,96,896]{2,1,0:T(8,128)(2,1)} %fusion.13.columns, bf16[3,6,96,256]{3,2,1,0:T(8,128)(2,1)} %bitcast_convert_fusion.fast_rows), custom_call_target="tpu_custom_call" | custom-call | flops 12079595520 | bytes 6291456 | tf_op jit(solution)/shard_map/pallas_call | solution.py:420
  226.3 0.0 copy-start.1
  226.4 1.9 fusion.12
  228.3 0.0 copy-done.1
  228.3 0.0 copy-start.2
  228.3 0.0 copy-start.3
  228.3 1.5 multiply_bitcast_fusion
  229.9 0.0 all-gather.3.cloned.1.call-done
  229.9 0.0 copy-done.2
  229.9 0.1 copy-done.3
  230.0 4.6 %fusion.8 = bf16[1,1,256,1536]{3,2,1,0:T(8,128)(2,1)} fusion(bf16[256,1536]{1,0:T(8,128)(2,1)S(1)} %copy-done.3, bf16[1,1536,1536]{2,1,0:T(8,128)(2,1)} %all-gather.3.cloned.1.call-done, bf16[256,1536]{1,0:T(8,128)(2,1)S(1)} %copy-done.2), kind=kOutput, calls=%fused_computation.4 | convolution fusion | flops 1209139200 | bytes 7077888 | tf_op jit(solution)/shard_map/dot_general | solution.py:452
  (1 shorter events, 0.0 us)
Async XLA Ops:
  7.2 222.7 %all-gather.3.cloned.1.call-start = ((), (), s32[]{:S(2)}) async-start(), calls=%async_computation | async-start | bytes 5013504 | tf_op jit(solution)/shard_map/all_gather | solution.py:404
  11.3 4.4 %copy-start = (f32[1,1,3,6,96,256]{5,4,3,2,1,0:T(8,128)S(1)}, f32[1,1,3,6,96,256]{5,4,3,2,1,0:T(8,128)}, u32[]{:S(2)}) copy-start(f32[1,1,3,6,96,256]{5,4,3,2,1,0:T(8,128)} %param.11) | copy-start | bytes 5308420
  226.3 2.0 copy-start.1
  228.3 1.6 copy-start.2
  228.3 1.6 copy-start.3
Sparse Core Ops, SparseCore 0:
  10.3 84.7 all-gather.2

commit v3 on v2

--- a/solution.py
+++ b/solution.py
@@ -16,7 +16,6 @@
 cubic_coef = -4.775
 quintic_coef = 2.0315
 update_scale = 8.0
-highest = lax.Precision.HIGHEST
 MESH = pl.DeviceIdType.MESH
 
 
@@ -28,22 +27,30 @@
     return values * lax.rsqrt(jnp.sum(values * values, axis=-1, keepdims=True) + 1e-06)
 
 
-def dot_nn(a, b, precision=None):
-    return jnp.dot(a, b, preferred_element_type=jnp.float32, precision=precision)
+def dot_nn(a, b):
+    return jnp.dot(a, b, preferred_element_type=jnp.float32)
 
 
 def dot_nt(a, b):
     return lax.dot_general(a, b, (((1,), (1,)), ((), ())), preferred_element_type=jnp.float32)
 
 
-def dot_tn(a, b, precision=None):
-    return lax.dot_general(
-        a, b, (((0,), (0,)), ((), ())), preferred_element_type=jnp.float32, precision=precision
-    )
+def dot_tn(a, b):
+    return lax.dot_general(a, b, (((0,), (0,)), ((), ())), preferred_element_type=jnp.float32)
+
+
+def parts_of(values):
+    high = values.astype(jnp.bfloat16)
+    return high, (values - high.astype(jnp.float32)).astype(jnp.bfloat16)
+
+
+def dot_split(dot, a, b):
+    return dot(a[0], b[0]) + (dot(a[0], b[1]) + dot(a[1], b[0]))
 
 
 def orthogonalize(gradient):
-    square = dot_tn(gradient, gradient, highest)
+    gradient_parts = parts_of(gradient)
+    square = dot_split(dot_tn, gradient_parts, gradient_parts)
     rows = lax.broadcasted_iota(jnp.int32, square.shape, 0)
     columns = lax.broadcasted_iota(jnp.int32, square.shape, 1)
     eye = (rows == columns).astype(jnp.float32)
@@ -52,12 +59,18 @@
     square = square * inverse_norm * inverse_norm
     total = None
     for iteration in range(NS_STEPS):
-        quad = dot_nn(square, square, highest)
+        square_parts = parts_of(square)
+        quad = dot_split(dot_nn, square_parts, square_parts)
         poly = linear_coef * eye + cubic_coef * square + quintic_coef * quad
-        total = poly if total is None else dot_nn(total, poly, highest)
+        poly_parts = parts_of(poly)
+        if total is None:
+            total = poly
+        else:
+            total = dot_split(dot_nn, parts_of(total), poly_parts)
         if iteration + 1 < NS_STEPS:
-            square = dot_nn(dot_nn(poly, square, highest), poly, highest)
-    return dot_nn(gradient * inverse_norm, total, highest)
+            left = dot_split(dot_nn, poly_parts, square_parts)
+            square = dot_split(dot_nn, parts_of(left), poly_parts)
+    return dot_split(dot_nn, gradient_parts, parts_of(total * inverse_norm))
 
 
 def block_terms(inputs, weight_ref, fast_ref, gradient_ref):
@@ -93,10 +106,11 @@
 
 
 def kernel(
-    sizes, fresh, carried, columns, fast_rows, inputs_out, head_out, update_out,
-    blocks, weight, fast, gradient, out_stage, out_land, update_stage, update_land,
+    sizes, fresh, carried, columns, fast_rows, out_rows, passed_out, update_out,
+    blocks, weight, fast, gradient, out_stage, out_land, update_stage, update_land, projection,
     y_sem, load_sem, own_sem, w_send, w_recv, f_send, f_recv, d_send, d_recv,
     up_send, down_send, line_recv, pair_send, pair_recv, h_send, h_recv, u_send, u_recv,
+    o_load, o_up_send, o_down_send, o_line_recv, o_pair_send, o_pair_recv, o_core_send, o_core_recv,
 ):
     n_ctx, n_sec, n_dp, heads = sizes
     lines = n_ctx // PAIR
@@ -182,6 +196,11 @@
         def _():
             f_copy(target).start()
 
+    def own_projection():
+        return pltpu.make_async_copy(out_rows.at[0], projection.at[me, dp], o_load)
+
+    own_projection().start()
+
     @pl.when(owner)
     def _():
         for copy in own_copies():
@@ -191,54 +210,85 @@
     def shard(row, which):
         return row * PAIR + which
 
-    def line_copy(row, sem, to_line):
-        at = shard(row, side)
-        return remote(
-            blocks.at[at], blocks.at[at], sem.at[row], line_recv.at[row],
-            ctx=shard(to_line, side),
-        )
-
-    def pair_copy(row):
-        at = shard(row, side)
-        return remote(
-            blocks.at[at], blocks.at[at], pair_send.at[row], pair_recv.at[row],
-            ctx=shard(line, 1 - side),
-        )
-
-    def pass_on(row, distance, sign):
+    def input_slot(at):
+        return blocks.at[at]
+
+    def projection_slot(at):
+        return projection.at[at, dp]
+
+    input_relay = (input_slot, up_send, down_send, line_recv, pair_send, pair_recv)
+    projection_relay = (
+        projection_slot, o_up_send, o_down_send, o_line_recv, o_pair_send, o_pair_recv
+    )
+
+    def up_copy(relay, row):
+        slot = relay[0](shard(row, side))
+        to = shard(lax.rem(line + 1, lines), side)
+        return remote(slot, slot, relay[1].at[row], relay[3].at[row], ctx=to)
+
+    def down_copy(relay, row):
+        slot = relay[0](shard(row, side))
+        to = shard(lax.rem(line + lines - 1, lines), side)
+        return remote(slot, slot, relay[2].at[row], relay[3].at[row], ctx=to)
+
+    def pair_copy(relay, row):
+        slot = relay[0](shard(row, side))
+        to = shard(line, 1 - side)
+        return remote(slot, slot, relay[4].at[row], relay[5].at[row], ctx=to)
+
+    def pair_arrived(relay, row):
+        slot = relay[0](shard(row, 1 - side))
+        to = shard(line, 1 - side)
+        remote(slot, slot, relay[4].at[row], relay[5].at[row], ctx=to).wait_recv()
+
+    def pass_on(relay, row, distance):
         @pl.when(distance > 0)
         def _():
-            remote(
-                blocks.at[shard(row, side)], blocks.at[shard(row, side)],
-                up_send.at[row], line_recv.at[row], ctx=peer(1),
-            ).wait_recv()
+            up_copy(relay, row).wait_recv()
 
         @pl.when((row <= line) & (line + 1 < lines))
         def _():
-            line_copy(row, up_send, line + 1).start()
+            up_copy(relay, row).start()
 
         @pl.when((row >= line) & (line > 0))
         def _():
-            line_copy(row, down_send, line - 1).start()
-
-        pair_copy(row).start()
+            down_copy(relay, row).start()
+
+        pair_copy(relay, row).start()
+
+    def relay_sent(relay):
+        for row in range(lines):
+            @pl.when((row <= line) & (line + 1 < lines))
+            def _():
+                up_copy(relay, row).wait_send()
+
+            @pl.when((row >= line) & (line > 0))
+            def _():
+                down_copy(relay, row).wait_send()
+
+            pair_copy(relay, row).wait_send()
 
     def out_copy(at):
         return remote(
             out_stage.at[at], out_land.at[me], h_send.at[at], h_recv.at[me], ctx=at
         )
 
-    def compute(at):
-        out = block_terms(blocks[at], weight, fast, gradient)
-
-        @pl.when(at == me)
-        def _():
-            out_land[me] = out
-
-        @pl.when(at != me)
-        def _():
-            out_stage[at] = out
-            out_copy(at).start()
+    def compute(row):
+        first = row * PAIR
+        tokens = blocks[pl.ds(first, PAIR)].reshape(PAIR * blocks.shape[1], blocks.shape[2])
+        out = block_terms(tokens, weight, fast, gradient)
+        for which in range(PAIR):
+            at = first + which
+            part = out[which * blocks.shape[1] : (which + 1) * blocks.shape[1]]
+
+            @pl.when(at == me)
+            def _():
+                out_land[me] = part
+
+            @pl.when(at != me)
+            def _():
+                out_stage[at] = part
+                out_copy(at).start()
 
     def rows_at(distance, sign):
         row = line + distance * (1 - 2 * sign)
@@ -291,60 +341,71 @@
 
                 @pl.when(valid)
                 def _():
-                    pass_on(row, distance, sign)
+                    pass_on(input_relay, row, distance)
 
         @pl.when(distance == 1)
         def _():
             weights_ready()
+            own_projection().wait()
 
         @pl.when(distance > 0)
         def _():
-            def block_body(index, inner):
-                sign, far = index // 2, lax.rem(index, 2)
+            def block_body(sign, inner):
                 row, valid = rows_at(distance - 1, sign)
 
                 @pl.when(valid)
                 def _():
-                    at = shard(row, lax.rem(side + far, 2))
-
-                    @pl.when(far == 1)
-                    def _():
-                        remote(
-                            blocks.at[at], blocks.at[at], pair_send.at[row], pair_recv.at[row],
-                            ctx=shard(line, 1 - side),
-                        ).wait_recv()
+                    pair_arrived(input_relay, row)
 
                     @pl.when(owner)
                     def _():
-                        compute(at)
+                        compute(row)
 
                 return inner
 
-            lax.fori_loop(0, 4, block_body, 0)
+            lax.fori_loop(0, 2, block_body, 0)
+
+            for sign in range(2):
+                row, valid = rows_at(distance - 1, sign)
+
+                @pl.when(valid)
+                def _():
+                    pass_on(projection_relay, row, distance - 1)
 
         return carry
 
     lax.fori_loop(0, lines + 1, step_body, 0)
 
-    def update_copy(target):
+    def core_copy(step):
+        return remote(
+            projection.at[:, dp], projection.at[:, dp], o_core_send.at[step], o_core_recv.at[step],
+            dp=lax.rem(dp + step, n_dp),
+        )
+
+
+    def update_copy(which, target):
         rows = pl.ds(pl.multiple_of(target * hidden_rows, hidden_rows), hidden_rows)
         return remote(
-            update_stage.at[:, rows], update_land.at[:, me], u_send.at[target], u_recv.at[me],
-            ctx=target,
+            update_stage.at[which, rows], update_land.at[which, me],
+            u_send.at[which, target], u_recv.at[which, me], ctx=target,
         )
 
     @pl.when(owner)
     def _():
         def matrix_body(which, carry):
             update_stage[which] = orthogonalize(gradient[which]).astype(jnp.bfloat16)
+            for step in range(1, n_ctx):
+                update_copy(which, peer(step)).start()
             return carry
 
         lax.fori_loop(0, 3, matrix_body, 0)
-        for step in range(1, n_ctx):
-            update_copy(peer(step)).start()
         update_land[:, me] = update_stage[:, my_rows]
 
-    inputs_out[...] = blocks[me]
+    for row in range(lines):
+        pair_arrived(projection_relay, row)
+    for step in range(1, n_dp):
+        core_copy(step).start()
+
     for head in range(heads):
         @pl.when(me != head)
         def _():
@@ -352,14 +413,25 @@
                 out_stage.at[0], out_land.at[head], h_send.at[0], h_recv.at[head], ctx=head
             ).wait_recv()
 
-        head_out[:, head * head_dim : (head + 1) * head_dim] = out_land[head]
-    for head in range(heads):
-        @pl.when(me != head)
-        def _():
-            remote(
-                update_stage.at[:, pl.ds(0, hidden_rows)], update_land.at[:, head],
-                u_send.at[0], u_recv.at[head], ctx=head,
-            ).wait_recv()
+    for step in range(1, n_dp):
+        source = lax.rem(dp + n_dp - step, n_dp)
+        remote(
+            projection.at[:, source], projection.at[:, source],
+            o_core_send.at[step], o_core_recv.at[step], dp=source,
+        ).wait()
+    head_out = jnp.concatenate([out_land[head] for head in range(heads)], axis=1)
+    full_out = projection[...].reshape(heads * head_dim, projection.shape[3])
+    branch_out = dot_nn(head_out, full_out)
+    passed_out[...] = (blocks[me].astype(jnp.float32) + branch_out).astype(jnp.bfloat16)
+
+    for which in range(3):
+        for head in range(heads):
+            @pl.when(me != head)
+            def _():
+                remote(
+                    update_stage.at[which, pl.ds(0, hidden_rows)], update_land.at[which, head],
+                    u_send.at[which, 0], u_recv.at[which, head], ctx=head,
+                ).wait_recv()
 
     update_out[...] = update_land[:, :heads]
 
@@ -378,18 +450,11 @@
         @pl.when(owner)
         def _():
             out_copy(target).wait_send()
-            update_copy(target).wait_send()
-
-    for row in range(lines):
-        @pl.when((row <= line) & (line + 1 < lines))
-        def _():
-            line_copy(row, up_send, lax.rem(line + 1, lines)).wait_send()
-
-        @pl.when((row >= line) & (line > 0))
-        def _():
-            line_copy(row, down_send, lax.rem(line + lines - 1, lines)).wait_send()
-
-        pair_copy(row).wait_send()
+            for which in range(3):
+                update_copy(which, target).wait_send()
+
+    relay_sent(input_relay)
+    relay_sent(projection_relay)
 
 
 def local(fresh_input, carried, qkv_weight, out_weight, rate_weight, fast_state):
@@ -401,7 +466,6 @@
     count, width = fresh_input.shape[1:]
     assert heads <= n_ctx and n_ctx % PAIR == 0
     previous = fast_state[0, 0]
-    full_out = lax.all_gather(out_weight[0], ("ctx", "dp"), axis=0, tiled=True)
 
     columns = qkv_weight[0].reshape(depth, 3, heads, head_dim).transpose(2, 0, 1, 3)
     columns = columns.reshape(heads, depth, 3 * head_dim)
@@ -417,15 +481,14 @@
     tokens = n_ctx * count
     hidden_all = n_ctx * hidden_rows
     flops = 2 * tokens * head_dim * (3 * width + 9 * hidden_all)
-    inputs, head_out, update = pl.pallas_call(
+    passed, update = pl.pallas_call(
         functools.partial(kernel, (n_ctx, n_sec, n_dp, heads)),
         out_shape=[
             jax.ShapeDtypeStruct((count, width), half),
-            jax.ShapeDtypeStruct((count, heads * head_dim), half),
             jax.ShapeDtypeStruct((3, heads, hidden_rows, head_dim), half),
         ],
-        in_specs=[any_spec] * 4,
-        out_specs=[vmem_spec] * 3,
+        in_specs=[any_spec] * 5,
+        out_specs=[vmem_spec] * 2,
         scratch_shapes=[
             pltpu.VMEM((n_ctx, count, width), half),
             pltpu.VMEM((n_ctx, n_dp, depth, 3 * head_dim + LANES), half),
@@ -435,11 +498,14 @@
             pltpu.VMEM((n_ctx, count, head_dim), half),
             pltpu.VMEM((3, hidden_all, head_dim), half),
             pltpu.VMEM((3, n_ctx, hidden_rows, head_dim), half),
+            pltpu.VMEM((n_ctx, n_dp, depth, width), half),
             dma((2,)), dma, dma((2,)),
             dma((n_ctx,)), dma((n_ctx,)), dma((n_ctx,)), dma((n_ctx,)),
             dma((n_dp,)), dma((n_dp,)),
             dma((lines,)), dma((lines,)), dma((lines,)), dma((lines,)), dma((lines,)),
-            dma((n_ctx,)), dma((n_ctx,)), dma((n_ctx,)), dma((n_ctx,)),
+            dma((n_ctx,)), dma((n_ctx,)), dma((3, n_ctx)), dma((3, n_ctx)),
+            dma, dma((lines,)), dma((lines,)), dma((lines,)), dma((lines,)), dma((lines,)),
+            dma((n_dp,)), dma((n_dp,)),
         ],
         compiler_params=pltpu.CompilerParams(
             collective_id=0, has_side_effects=True, vmem_limit_bytes=VMEM_BYTES
@@ -447,10 +513,8 @@
         cost_estimate=pl.CostEstimate(
             flops=flops, bytes_accessed=tokens * width * 2, transcendentals=4 * tokens * hidden_all
         ),
-    )(fresh_input, carried, columns, fast_rows)
-
-    branch_out = jnp.dot(head_out, full_out, preferred_element_type=jnp.float32)
-    passed = (inputs.astype(jnp.float32) + branch_out).astype(jnp.bfloat16)
+    )(fresh_input, carried, columns, fast_rows, out_weight)
+
     stepped = previous - update_scale * update.astype(jnp.float32)
     rescale = jnp.sqrt(jnp.mean(previous * previous, axis=-1, keepdims=True) + 1e-06) * lax.rsqrt(
         jnp.mean(stepped * stepped, axis=-1, keepdims=True) + 1e-06

time: 243 us -> 198 us (0.81)
  Pallas kernels: 210 us -> 186 us
  between operations: 14.1 us -> 0.71 us
  matrix products: 4.6 us -> 0 us
    pallas_call x1, Pallas kernels: 210 us -> 186 us  [local(): pl.pallas_call(functools.partial(kernel, (n_ctx, n_sec, n_dp, heads)), ou...]
    dot_general x1 -> x0, matrix products: 4.6 us -> none  [local(): branch_out = jnp.dot(head_out, full_out, preferred_element_type=jnp.float32)]
  transfers between devices with their start and end apart: 1 -> 0, of which waited for: 0 -> 0; matrix products, arithmetic and copies ran while one was open for 5% -> 0% of each run, Pallas kernels for 87% -> 0%
where the time goes in v3:
time: 198 us
  Pallas kernels  186 us (94%)
  other arithmetic  7.04 us (4%)
  local copies, waits for them, and re-layouts  4.33 us (2%)
    pallas_call x1, Pallas kernels, local(): pl.pallas_call(functools.partial(kernel, (n_ctx, n_sec, n_dp, heads)), ou...  186 us

profile of v3, /device:TPU:24, one launch (start us, length us, event | category | flops | bytes accessed | tf_op | source)
XLA Modules:
  0.0 198.1 jit_solution(6663246389964149143)
XLA Ops:
  0.6 0.0 copy-start.2
  0.6 0.9 copy.10
  1.6 2.5 %bitcast_convert_fusion.fast_rows = bf16[3,6,96,256]{3,2,1,0:T(8,128)(2,1)} fusion(f32[1,1,3,6,96,256]{5,4,3,2,1,0:T(8,128)} %param.11), kind=kLoop, calls=%fused_computation.4 | loop fusion | flops 442368 | bytes 2654208 | tf_op jit(solution)/shard_map/convert_element_type | solution.py:474
  4.1 0.0 copy-done.2
  4.1 1.0 reshape_squeeze.3
  5.1 0.5 copy.9
  5.6 1.1 reshape.25
  6.6 1.0 fusion.2.columns
  7.7 0.0 copy-start
  7.7 186.0 %shard_map.77 = (bf16[256,1536]{1,0:T(8,128)(2,1)}, bf16[3,6,96,256]{3,2,1,0:T(8,128)(2,1)}) custom-call(bf16[1,256,1536]{2,1,0:T(8,128)(2,1)} %fresh.1, bf16[1,1,256,1536]{3,2,1,0:T(8,128)(2,1)} %carried.1, bf16[6,96,896]{2,1,0:T(8,128)(2,1)} %fusion.2.columns, bf16[3,6,96,256]{3,2,1,0:T(8,128)(2,1)} %bitcast_convert_fusion.fast_rows, ...), custom_call_target="tpu_custom_call" | custom-call | flops 12079595520 | bytes 6291456 | tf_op jit(solution)/shard_map/pallas_call | solution.py:484
  193.6 0.0 copy-start.1
  193.6 0.0 copy-done
  193.7 1.9 fusion.1
  195.6 0.0 copy-done.1
  195.6 0.0 copy-start.3
  195.6 1.5 multiply_bitcast_fusion
  197.2 0.0 copy-done.3
  197.2 0.9 copy.12
  (1 shorter events, 0.0 us)
Async XLA Ops:
  0.6 3.5 %copy-start.2 = (bf16[1,96,4608]{2,1,0:T(8,128)(2,1)S(1)}, bf16[1,96,4608]{2,1,0:T(8,128)(2,1)}, u32[]{:S(2)}) copy-start(bf16[1,96,4608]{2,1,0:T(8,128)(2,1)} %param.8) | copy-start | bytes 2654212
  7.7 186.0 %copy-start = (f32[1,1,3,6,96,256]{5,4,3,2,1,0:T(8,128)S(1)}, f32[1,1,3,6,96,256]{5,4,3,2,1,0:T(8,128)}, u32[]{:S(2)}) copy-start(f32[1,1,3,6,96,256]{5,4,3,2,1,0:T(8,128)} %param.11) | copy-start | bytes 5308420
  193.6 2.0 copy-start.1
  195.6 1.6 copy-start.3

commit v4 on v3

--- a/solution.py
+++ b/solution.py
@@ -346,7 +346,11 @@
         @pl.when(distance == 1)
         def _():
             weights_ready()
+
+        @pl.when(distance == lines - 1)
+        def _():
             own_projection().wait()
+            pass_on(projection_relay, line, 0)
 
         @pl.when(distance > 0)
         def _():
@@ -365,16 +369,17 @@
 
             lax.fori_loop(0, 2, block_body, 0)
 
-            for sign in range(2):
-                row, valid = rows_at(distance - 1, sign)
-
-                @pl.when(valid)
-                def _():
-                    pass_on(projection_relay, row, distance - 1)
-
         return carry
 
     lax.fori_loop(0, lines + 1, step_body, 0)
+
+    def projection_step(distance):
+        for sign in range(2):
+            row, valid = rows_at(distance, sign)
+
+            @pl.when(valid)
+            def _():
+                pass_on(projection_relay, row, distance)
 
     def core_copy(step):
         return remote(
@@ -390,15 +395,26 @@
             u_send.at[which, target], u_recv.at[which, me], ctx=target,
         )
 
-    @pl.when(owner)
-    def _():
-        def matrix_body(which, carry):
+    def matrix_body(which, carry):
+        projection_step(which + 1)
+
+        @pl.when(owner)
+        def _():
             update_stage[which] = orthogonalize(gradient[which]).astype(jnp.bfloat16)
             for step in range(1, n_ctx):
                 update_copy(which, peer(step)).start()
-            return carry
-
-        lax.fori_loop(0, 3, matrix_body, 0)
+
+        return carry
+
+    def rest_body(distance, carry):
+        projection_step(distance)
+        return carry
+
+    lax.fori_loop(0, 3, matrix_body, 0)
+    lax.fori_loop(4, max(lines, 4), rest_body, 0)
+
+    @pl.when(owner)
+    def _():
         update_land[:, me] = update_stage[:, my_rows]
 
     for row in range(lines):

time: 198 us -> 211 us (1.066)
  Pallas kernels: 186 us -> 197 us
    pallas_call x1, Pallas kernels: 186 us -> 197 us  [local(): pl.pallas_call(functools.partial(kernel, (n_ctx, n_sec, n_dp, heads)), ou...]
where the time goes in v4:
time: 211 us; the launch traced here: 209 us
  Pallas kernels  197 us (93%)
  other arithmetic  7.04 us (3%)
  local copies, waits for them, and re-layouts  4.33 us (2%)
    pallas_call x1, Pallas kernels, local(): pl.pallas_call(functools.partial(kernel, (n_ctx, n_sec, n_dp, heads)), ou...  197 us

profile of v4, /device:TPU:24, one launch (start us, length us, event | category | flops | bytes accessed | tf_op | source)
XLA Modules:
  0.0 209.2 jit_solution(4866875107896820173)
XLA Ops:
  0.6 0.0 copy-start.2
  0.6 0.9 copy.10
  1.6 2.5 %bitcast_convert_fusion.fast_rows = bf16[3,6,96,256]{3,2,1,0:T(8,128)(2,1)} fusion(f32[1,1,3,6,96,256]{5,4,3,2,1,0:T(8,128)} %param.11), kind=kLoop, calls=%fused_computation.4 | loop fusion | flops 442368 | bytes 2654208 | tf_op jit(solution)/shard_map/convert_element_type | solution.py:490
  4.1 0.0 copy-done.2
  4.1 1.0 reshape_squeeze.3
  5.1 0.5 copy.9
  5.6 1.1 reshape.25
  6.6 1.0 fusion.2.columns
  7.7 0.0 copy-start
  7.7 197.1 %shard_map.77 = (bf16[256,1536]{1,0:T(8,128)(2,1)}, bf16[3,6,96,256]{3,2,1,0:T(8,128)(2,1)}) custom-call(bf16[1,256,1536]{2,1,0:T(8,128)(2,1)} %fresh.1, bf16[1,1,256,1536]{3,2,1,0:T(8,128)(2,1)} %carried.1, bf16[6,96,896]{2,1,0:T(8,128)(2,1)} %fusion.2.columns, bf16[3,6,96,256]{3,2,1,0:T(8,128)(2,1)} %bitcast_convert_fusion.fast_rows, ...), custom_call_target="tpu_custom_call" | custom-call | flops 12079595520 | bytes 6291456 | tf_op jit(solution)/shard_map/pallas_call | solution.py:500
  204.7 0.0 copy-start.1
  204.7 0.0 copy-done
  204.7 1.9 fusion.1
  206.7 0.0 copy-done.1
  206.7 0.0 copy-start.3
  206.7 1.5 multiply_bitcast_fusion
  208.3 0.0 copy-done.3
  208.3 0.9 copy.12
  (1 shorter events, 0.0 us)
Async XLA Ops:
  0.6 3.5 %copy-start.2 = (bf16[1,96,4608]{2,1,0:T(8,128)(2,1)S(1)}, bf16[1,96,4608]{2,1,0:T(8,128)(2,1)}, u32[]{:S(2)}) copy-start(bf16[1,96,4608]{2,1,0:T(8,128)(2,1)} %param.8) | copy-start | bytes 2654212
  7.7 197.1 %copy-start = (f32[1,1,3,6,96,256]{5,4,3,2,1,0:T(8,128)S(1)}, f32[1,1,3,6,96,256]{5,4,3,2,1,0:T(8,128)}, u32[]{:S(2)}) copy-start(f32[1,1,3,6,96,256]{5,4,3,2,1,0:T(8,128)} %param.11) | copy-start | bytes 5308420
  204.7 2.0 copy-start.1
  206.7 1.6 copy-start.3

commit v5 on v3

--- a/solution.py
+++ b/solution.py
@@ -10,6 +10,7 @@
 NS_STEPS = 2
 LANES = 128
 PAIR = 2
+CHUNKS = 2
 VMEM_BYTES = 56 * 2**20
 
 linear_coef = 3.4445
@@ -147,9 +148,13 @@
         )
     pl.semaphore_wait(barrier, n_ctx + n_dp + n_sec - 3)
 
-    def y_copy():
+    part = blocks.shape[1] // CHUNKS
+
+    def y_copy(chunk):
+        rows = pl.ds(chunk * part, part)
         return remote(
-            carried.at[0, 0], blocks.at[me], y_sem.at[0], y_sem.at[1], sec=lax.rem(sec + 1, n_sec)
+            carried.at[0, 0, rows], blocks.at[me, rows], y_sem.at[0, chunk], y_sem.at[1, chunk],
+            sec=lax.rem(sec + 1, n_sec),
         )
 
     def fresh_copy():
@@ -157,7 +162,8 @@
 
     @pl.when(to_sec)
     def _():
-        y_copy().start()
+        for chunk in range(CHUNKS):
+            y_copy(chunk).start()
 
     @pl.when(sec == 0)
     def _():
@@ -210,13 +216,18 @@
     def shard(row, which):
         return row * PAIR + which
 
-    def input_slot(at):
-        return blocks.at[at]
+    def input_relay(chunk):
+        def slot(at):
+            return blocks.at[at, pl.ds(chunk * part, part)]
+
+        sems = (up_send, down_send, line_recv, pair_send, pair_recv)
+        return (slot,) + tuple(sem.at[chunk] for sem in sems)
+
+    input_relays = [input_relay(chunk) for chunk in range(CHUNKS)]
 
     def projection_slot(at):
         return projection.at[at, dp]
 
-    input_relay = (input_slot, up_send, down_send, line_recv, pair_send, pair_recv)
     projection_relay = (
         projection_slot, o_up_send, o_down_send, o_line_recv, o_pair_send, o_pair_recv
     )
@@ -298,10 +309,6 @@
     @pl.when(sec == 0)
     def _():
         fresh_copy().wait()
-
-    @pl.when(from_sec)
-    def _():
-        y_copy().wait_recv()
 
     def weights_ready():
         @pl.when(owner)
@@ -336,26 +343,32 @@
     def step_body(distance, carry):
         @pl.when(distance < lines)
         def _():
-            for sign in range(2):
-                row, valid = rows_at(distance, sign)
+            for chunk, relay in enumerate(input_relays):
+                @pl.when(from_sec & (distance == 0))
+                def _():
+                    y_copy(chunk).wait_recv()
+
+                for sign in range(2):
+                    row, valid = rows_at(distance, sign)
+
+                    @pl.when(valid)
+                    def _():
+                        pass_on(relay, row, distance)
+
+        @pl.when(distance == 1)
+        def _():
+            weights_ready()
+            own_projection().wait()
+
+        @pl.when(distance > 0)
+        def _():
+            def block_body(sign, inner):
+                row, valid = rows_at(distance - 1, sign)
 
                 @pl.when(valid)
                 def _():
-                    pass_on(input_relay, row, distance)
-
-        @pl.when(distance == 1)
-        def _():
-            weights_ready()
-            own_projection().wait()
-
-        @pl.when(distance > 0)
-        def _():
-            def block_body(sign, inner):
-                row, valid = rows_at(distance - 1, sign)
-
-                @pl.when(valid)
-                def _():
-                    pair_arrived(input_relay, row)
+                    for relay in input_relays:
+                        pair_arrived(relay, row)
 
                     @pl.when(owner)
                     def _():
@@ -437,7 +450,8 @@
 
     @pl.when(to_sec)
     def _():
-        y_copy().wait_send()
+        for chunk in range(CHUNKS):
+            y_copy(chunk).wait_send()
 
     for step in range(1, n_ctx):
         target = peer(step)
@@ -453,7 +467,8 @@
             for which in range(3):
                 update_copy(which, target).wait_send()
 
-    relay_sent(input_relay)
+    for relay in input_relays:
+        relay_sent(relay)
     relay_sent(projection_relay)
 
 
@@ -499,10 +514,11 @@
             pltpu.VMEM((3, hidden_all, head_dim), half),
             pltpu.VMEM((3, n_ctx, hidden_rows, head_dim), half),
             pltpu.VMEM((n_ctx, n_dp, depth, width), half),
-            dma((2,)), dma, dma((2,)),
+            dma((2, CHUNKS)), dma, dma((2,)),
             dma((n_ctx,)), dma((n_ctx,)), dma((n_ctx,)), dma((n_ctx,)),
             dma((n_dp,)), dma((n_dp,)),
-            dma((lines,)), dma((lines,)), dma((lines,)), dma((lines,)), dma((lines,)),
+            dma((CHUNKS, lines)), dma((CHUNKS, lines)), dma((CHUNKS, lines)),
+            dma((CHUNKS, lines)), dma((CHUNKS, lines)),
             dma((n_ctx,)), dma((n_ctx,)), dma((3, n_ctx)), dma((3, n_ctx)),
             dma, dma((lines,)), dma((lines,)), dma((lines,)), dma((lines,)), dma((lines,)),
             dma((n_dp,)), dma((n_dp,)),

time: 198 us -> 187 us (0.944)
  Pallas kernels: 186 us -> 175 us
    pallas_call x1, Pallas kernels: 186 us -> 175 us  [local(): pl.pallas_call(functools.partial(kernel, (n_ctx, n_sec, n_dp, heads)), ou...]
where the time goes in v5:
time: 187 us
  Pallas kernels  175 us (94%)
  other arithmetic  7.04 us (4%)
  local copies, waits for them, and re-layouts  4.33 us (2%)
    pallas_call x1, Pallas kernels, local(): pl.pallas_call(functools.partial(kernel, (n_ctx, n_sec, n_dp, heads)), ou...  175 us

profile of v5, /device:TPU:24, one launch (start us, length us, event | category | flops | bytes accessed | tf_op | source)
XLA Modules:
  0.0 187.2 jit_solution(5043960311281528999)
XLA Ops:
  0.6 0.0 copy-start.2
  0.6 0.9 copy.10
  1.6 2.5 %bitcast_convert_fusion.fast_rows = bf16[3,6,96,256]{3,2,1,0:T(8,128)(2,1)} fusion(f32[1,1,3,6,96,256]{5,4,3,2,1,0:T(8,128)} %param.11), kind=kLoop, calls=%fused_computation.4 | loop fusion | flops 442368 | bytes 2654208 | tf_op jit(solution)/shard_map/convert_element_type | solution.py:489
  4.1 0.0 copy-done.2
  4.1 1.0 reshape_squeeze.3
  5.1 0.5 copy.9
  5.6 1.1 reshape.25
  6.6 1.0 fusion.2.columns
  7.7 0.0 copy-start
  7.7 175.2 %shard_map.77 = (bf16[256,1536]{1,0:T(8,128)(2,1)}, bf16[3,6,96,256]{3,2,1,0:T(8,128)(2,1)}) custom-call(bf16[1,256,1536]{2,1,0:T(8,128)(2,1)} %fresh.1, bf16[1,1,256,1536]{3,2,1,0:T(8,128)(2,1)} %carried.1, bf16[6,96,896]{2,1,0:T(8,128)(2,1)} %fusion.2.columns, bf16[3,6,96,256]{3,2,1,0:T(8,128)(2,1)} %bitcast_convert_fusion.fast_rows, ...), custom_call_target="tpu_custom_call" | custom-call | flops 12079595520 | bytes 6291456 | tf_op jit(solution)/shard_map/pallas_call | solution.py:499
  182.8 0.0 copy-start.1
  182.8 0.0 copy-done
  182.8 1.9 %fusion.1 = (f32[3,6,96]{2,1,0:T(8,128)S(1)}, f32[3,6,96]{2,1,0:T(8,128)S(1)}) fusion(f32[1,1,3,6,96,256]{5,4,3,2,1,0:T(8,128)S(1)} %copy-done, bf16[3,6,96,256]{3,2,1,0:T(8,128)(2,1)} %get-tuple-element.5), kind=kLoop, calls=%fused_computation.5 | loop fusion | flops 3093120 | bytes 2668032 | tf_op jit(solution)/shard_map/reduce_sum | solution.py:535
  184.8 0.0 copy-done.1
  184.8 0.0 copy-start.3
  184.8 1.5 multiply_bitcast_fusion
  186.4 0.0 copy-done.3
  186.4 0.9 copy.12
  (1 shorter events, 0.0 us)
Async XLA Ops:
  0.6 3.5 %copy-start.2 = (bf16[1,96,4608]{2,1,0:T(8,128)(2,1)S(1)}, bf16[1,96,4608]{2,1,0:T(8,128)(2,1)}, u32[]{:S(2)}) copy-start(bf16[1,96,4608]{2,1,0:T(8,128)(2,1)} %param.8) | copy-start | bytes 2654212
  7.7 175.2 %copy-start = (f32[1,1,3,6,96,256]{5,4,3,2,1,0:T(8,128)S(1)}, f32[1,1,3,6,96,256]{5,4,3,2,1,0:T(8,128)}, u32[]{:S(2)}) copy-start(f32[1,1,3,6,96,256]{5,4,3,2,1,0:T(8,128)} %param.11) | copy-start | bytes 5308420
  182.8 2.0 %copy-start.1 = (bf16[3,6,96,256]{3,2,1,0:T(8,128)(2,1)S(1)}, bf16[3,6,96,256]{3,2,1,0:T(8,128)(2,1)}, u32[]{:S(2)}) copy-start(bf16[3,6,96,256]{3,2,1,0:T(8,128)(2,1)} %get-tuple-element.5) | copy-start | bytes 2654212
  184.8 1.6 copy-start.3

commit v6 on v5

--- a/solution.py
+++ b/solution.py
@@ -10,7 +10,7 @@
 NS_STEPS = 2
 LANES = 128
 PAIR = 2
-CHUNKS = 2
+CHUNKS = 4
 VMEM_BYTES = 56 * 2**20
 
 linear_coef = 3.4445
@@ -121,7 +121,8 @@
     line, side = me // PAIR, lax.rem(me, PAIR)
     hidden_rows = fast_rows.shape[2]
     head_dim = fast_rows.shape[3]
-    owner = me < heads
+    shift = (n_ctx - heads) // 2
+    owner = (me >= shift) & (me < shift + heads)
     from_sec = sec > 0
     to_sec = sec + 1 < n_sec
 
@@ -173,32 +174,32 @@
 
     def w_copy(target):
         return remote(
-            columns.at[target], weight.at[me, dp], w_send.at[target], w_recv.at[me], ctx=target
+            columns.at[target - shift], weight.at[me, dp], w_send.at[target], w_recv.at[me], ctx=target
         )
 
     def f_copy(target):
         return remote(
-            fast_rows.at[:, target], fast.at[:, my_rows], f_send.at[target], f_recv.at[me],
+            fast_rows.at[:, target - shift], fast.at[:, my_rows], f_send.at[target], f_recv.at[me],
             ctx=target,
         )
 
     def own_copies():
         return (
-            pltpu.make_async_copy(columns.at[me], weight.at[me, dp], own_sem.at[0]),
-            pltpu.make_async_copy(fast_rows.at[:, me], fast.at[:, my_rows], own_sem.at[1]),
+            pltpu.make_async_copy(columns.at[me - shift], weight.at[me, dp], own_sem.at[0]),
+            pltpu.make_async_copy(fast_rows.at[:, me - shift], fast.at[:, my_rows], own_sem.at[1]),
         )
 
     for step in range(1, n_ctx):
         target = peer(step)
 
-        @pl.when(target < heads)
+        @pl.when((target >= shift) & (target < shift + heads))
         def _():
             w_copy(target).start()
 
     for step in range(1, n_ctx):
         target = peer(step)
 
-        @pl.when(target < heads)
+        @pl.when((target >= shift) & (target < shift + heads))
         def _():
             f_copy(target).start()
 
@@ -419,7 +420,7 @@
     for step in range(1, n_dp):
         core_copy(step).start()
 
-    for head in range(heads):
+    for head in range(shift, shift + heads):
         @pl.when(me != head)
         def _():
             remote(
@@ -432,13 +433,13 @@
             projection.at[:, source], projection.at[:, source],
             o_core_send.at[step], o_core_recv.at[step], dp=source,
         ).wait()
-    head_out = jnp.concatenate([out_land[head] for head in range(heads)], axis=1)
+    head_out = jnp.concatenate([out_land[shift + head] for head in range(heads)], axis=1)
     full_out = projection[...].reshape(heads * head_dim, projection.shape[3])
     branch_out = dot_nn(head_out, full_out)
     passed_out[...] = (blocks[me].astype(jnp.float32) + branch_out).astype(jnp.bfloat16)
 
     for which in range(3):
-        for head in range(heads):
+        for head in range(shift, shift + heads):
             @pl.when(me != head)
             def _():
                 remote(
@@ -446,7 +447,7 @@
                     u_send.at[which, 0], u_recv.at[which, head], ctx=head,
                 ).wait_recv()
 
-    update_out[...] = update_land[:, :heads]
+    update_out[...] = update_land[:, shift : shift + heads]
 
     @pl.when(to_sec)
     def _():
@@ -456,7 +457,7 @@
     for step in range(1, n_ctx):
         target = peer(step)
 
-        @pl.when(target < heads)
+        @pl.when((target >= shift) & (target < shift + heads))
         def _():
             w_copy(target).wait_send()
             f_copy(target).wait_send()

time: 187 us -> 181 us (0.968)
  the two profiles are of different devices: /device:TPU:24 before, /device:TPU:3 now
where the time goes in v6:
time: 181 us; the launch traced here: 180 us
  Pallas kernels  168 us (93%)
  other arithmetic  7.04 us (4%)
  local copies, waits for them, and re-layouts  4.33 us (2%)
    pallas_call x1, Pallas kernels, local(): pl.pallas_call(functools.partial(kernel, (n_ctx, n_sec, n_dp, heads)), ou...  168 us

profile of v6, /device:TPU:3, one launch (start us, length us, event | category | flops | bytes accessed | tf_op | source)
XLA Modules:
  0.0 180.4 jit_solution(2109554462007849943)
XLA Ops:
  0.6 0.0 copy-start.2
  0.6 0.9 copy.10
  1.6 2.5 %bitcast_convert_fusion.fast_rows = bf16[3,6,96,256]{3,2,1,0:T(8,128)(2,1)} fusion(f32[1,1,3,6,96,256]{5,4,3,2,1,0:T(8,128)} %param.11), kind=kLoop, calls=%fused_computation.4 | loop fusion | flops 442368 | bytes 2654208 | tf_op jit(solution)/shard_map/convert_element_type | solution.py:490
  4.1 0.0 copy-done.2
  4.1 1.0 reshape_squeeze.3
  5.1 0.5 copy.9
  5.6 1.1 reshape.25
  6.6 1.0 fusion.2.columns
  7.7 0.0 copy-start
  7.7 168.3 %shard_map.77 = (bf16[256,1536]{1,0:T(8,128)(2,1)}, bf16[3,6,96,256]{3,2,1,0:T(8,128)(2,1)}) custom-call(bf16[1,256,1536]{2,1,0:T(8,128)(2,1)} %fresh.1, bf16[1,1,256,1536]{3,2,1,0:T(8,128)(2,1)} %carried.1, bf16[6,96,896]{2,1,0:T(8,128)(2,1)} %fusion.2.columns, bf16[3,6,96,256]{3,2,1,0:T(8,128)(2,1)} %bitcast_convert_fusion.fast_rows, ...), custom_call_target="tpu_custom_call" | custom-call | flops 12079595520 | bytes 6291456 | tf_op jit(solution)/shard_map/pallas_call | solution.py:500
  176.0 0.0 copy-start.1
  176.0 0.0 copy-done
  176.0 1.9 %fusion.1 = (f32[3,6,96]{2,1,0:T(8,128)S(1)}, f32[3,6,96]{2,1,0:T(8,128)S(1)}) fusion(f32[1,1,3,6,96,256]{5,4,3,2,1,0:T(8,128)S(1)} %copy-done, bf16[3,6,96,256]{3,2,1,0:T(8,128)(2,1)} %get-tuple-element.5), kind=kLoop, calls=%fused_computation.5 | loop fusion | flops 3093120 | bytes 2668032 | tf_op jit(solution)/shard_map/reduce_sum | solution.py:536
  178.0 0.0 copy-done.1
  178.0 0.0 copy-start.3
  178.0 1.5 multiply_bitcast_fusion
  179.5 0.0 copy-done.3
  179.5 0.9 copy.12
  (1 shorter events, 0.0 us)
Async XLA Ops:
  0.6 3.5 %copy-start.2 = (bf16[1,96,4608]{2,1,0:T(8,128)(2,1)S(1)}, bf16[1,96,4608]{2,1,0:T(8,128)(2,1)}, u32[]{:S(2)}) copy-start(bf16[1,96,4608]{2,1,0:T(8,128)(2,1)} %param.8) | copy-start | bytes 2654212
  7.7 168.3 %copy-start = (f32[1,1,3,6,96,256]{5,4,3,2,1,0:T(8,128)S(1)}, f32[1,1,3,6,96,256]{5,4,3,2,1,0:T(8,128)}, u32[]{:S(2)}) copy-start(f32[1,1,3,6,96,256]{5,4,3,2,1,0:T(8,128)} %param.11) | copy-start | bytes 5308420
  176.0 2.0 %copy-start.1 = (bf16[3,6,96,256]{3,2,1,0:T(8,128)(2,1)S(1)}, bf16[3,6,96,256]{3,2,1,0:T(8,128)(2,1)}, u32[]{:S(2)}) copy-start(bf16[3,6,96,256]{3,2,1,0:T(8,128)(2,1)} %get-tuple-element.5) | copy-start | bytes 2654212
  178.0 1.6 copy-start.3
